TPU v7x, 32 devices: a whole 2x2x4 slice. The times are simulated.
32 devices in a mesh: row: 4 (over y, x), col: 8 (over z, core).
Axes of the slice: x: 2, y: 2, z: 4, core: 2. Of those that a mesh axis runs over, the one named last changes fastest.
Arguments:
- features: float32 [8192, 512], P(('col', 'row')), may hold values from -6 to 6
- weight: float32 [512, 512], replicated, may hold values from -0.25 to 0.25
- tile_values: bfloat16 [4, 8, 32, 256, 256], P('row', 'col'), as said below
- tile_ids: int32 [4, 8, 32, 2], P('row', 'col'), may hold values from 0 to 7, as said below
- tile_counts: int32 [4, 8], P('row', 'col'), may hold values from 1 to 32, as said below
Outputs:
- activated: float32 [8192, 512], P(('row', 'col'))
Inputs may be any that keep to these rules, and one draw needn't show every extreme that they name: `tile_counts`: slots at or beyond a panel's count are ignored; some panel holds 32 live slots. `tile_ids`: the first entry is below 8, the second below 4; a tile may repeat. `tile_values`: nonnegative.
All inputs are finite; a program needn't handle non-finite values.
Results may differ from a plain program's by a relative error of at most 0.0003.
Values may be sent and summed in bfloat16 or wider, within the bound.
A program may use at most 128 MiB of HBM per device.

v0:
```python
import jax
import jax.numpy as jnp
from jax import lax
from jax.sharding import PartitionSpec as P


def shards(features, weight, tile_values, tile_ids, tile_counts):
    tile_set = tile_values[0, 0]
    tile_slots = tile_ids[0, 0]
    live_count = tile_counts[0, 0]
    tile_size = tile_set.shape[1]
    slot_total = tile_set.shape[0]
    grid_row = lax.axis_index("row")
    column_in_grid = lax.axis_index("col")
    own_rows = features.shape[0]
    panel_cols = own_rows * lax.axis_size("row")
    panel_rows = own_rows * lax.axis_size("col")
    row_blocks = panel_rows // tile_size
    width = features.shape[1]

    def unchanged(state):
        return state

    is_live = (jnp.arange(slot_total) < live_count).astype(jnp.float32)
    tile_sums = jnp.sum(tile_set, axis=2, dtype=jnp.float32)
    placement = (tile_slots[:, 0][:, None] == jnp.arange(row_blocks)[None, :]).astype(
        jnp.float32
    ) * is_live[:, None]
    row_sums = jnp.dot(placement.T, tile_sums, precision=lax.Precision.HIGHEST).reshape(panel_rows)
    weighted = jnp.dot(features, weight, precision=lax.Precision.HIGHEST)
    empty = jnp.zeros((panel_rows, width), jnp.float32)
    partial_value = empty
    shard_rows = lax.all_gather(weighted, "row", axis=0, tiled=True)
    length = shard_rows.shape[0]

    def one_tile(slot_index, current):
        row_blk = tile_slots[slot_index, 0]
        col_offset = tile_slots[slot_index, 1] * tile_size
        inside = (slot_index < live_count) & (col_offset >= 0) & (col_offset + tile_size <= length)

        def add_tile(state):
            columns = lax.dynamic_slice_in_dim(shard_rows, col_offset, tile_size, 0)
            product = jnp.dot(
                tile_set[slot_index].astype(jnp.float32), columns, precision=lax.Precision.HIGHEST
            )
            old_rows = lax.dynamic_slice_in_dim(state, row_blk * tile_size, tile_size, 0)
            return lax.dynamic_update_slice_in_dim(
                state, old_rows + product, row_blk * tile_size, 0
            )

        return lax.cond(inside, add_tile, unchanged, current)

    partial_value = lax.fori_loop(0, slot_total, one_tile, partial_value)

    def one_self(block_index, current):
        global_blk = column_in_grid * panel_cols // tile_size + block_index
        row_blk = global_blk - grid_row * row_blocks
        inside = (row_blk >= 0) & (row_blk < row_blocks)

        def add_self(state):
            own_block = lax.dynamic_slice_in_dim(shard_rows, block_index * tile_size, tile_size, 0)
            old_rows = lax.dynamic_slice_in_dim(state, row_blk * tile_size, tile_size, 0)
            return lax.dynamic_update_slice_in_dim(
                state, old_rows + own_block, row_blk * tile_size, 0
            )

        return lax.cond(inside, add_self, unchanged, current)

    folded = lax.fori_loop(0, length // tile_size, one_self, partial_value)
    partial_value = folded
    own_share, degree_part = (
        lax.psum_scatter(partial_value, "col", scatter_dimension=0, tiled=True),
        lax.psum_scatter(row_sums, "col", scatter_dimension=0, tiled=True),
    )
    inverse_root = lax.rsqrt(1.0 + degree_part)
    return jnp.maximum(own_share * inverse_root[:, None], 0.0)


def solution(mesh):
    in_specs = (
        P(("col", "row"), None),
        P(),
        P("row", "col", None, None, None),
        P("row", "col", None, None),
        P("row", "col"),
    )
    out_specs = P(("row", "col"), None)
    return jax.shard_map(shards, mesh=mesh, in_specs=in_specs, out_specs=out_specs, check_vma=False)
```

profile of v0, /device:TPU:0, one launch (start us, length us, event | category | flops | bytes accessed | tf_op | source)
XLA Modules:
  0.0 410.3 jit_solution(164830195904009345)
XLA Ops:
  6.5 1.2 copy-done
  7.8 2.9 fusion.13
  10.7 38.1 %all-gather.2.cloned.1.call-done = f32[1024,512]{1,0:T(8,128)} async-done(((f32[256,512]{1,0:T(8,128)}), f32[1024,512]{1,0:T(8,128)}) %all-gather.2.cloned.1.call-update) | async-done | bytes 2097168 | tf_op jit(solution)/shard_map/all_gather | solution.py:33
  48.8 2.5 broadcast_in_dim.2
  51.3 102.7 %while.35 = (s32[]{:T(128)}, f32[2048,512]{1,0:T(8,128)}, s32[]{:T(128)}, s32[32,2]{0,1:T(2,128)S(1)}, bf16[32,256,256]{2,1,0:T(8,128)(2,1)}, /*index=5*/f32[102...) while((s32[]{:T(128)}, f32[2048,512]{1,0:T(8,128)}, s32[]{:T(128)}, s32[32,2]{0,1:T(2,128)S(1)}, ...), condition=%wide.region_3.4_spmd, body=%wide.region_0.3_spmd.sunk | while | flops 402784256 | bytes 1704281 | solution.py:53
  53.9 6.8 %conditional.4 = (f32[2048,512]{1,0:T(8,128)}) conditional(s32[]{:T(128)} %convert_element_type.35, f32[2048,512]{1,0:T(8,128)} %get-tuple-element.475, (s32[32,2]{0,1:T(2,128)S(1)}, s32[]{:T(128)}, f32[2048,512]{1,0:T(8,128)}, bf16[32,256,256]{2,1,0:T(8,128)(2,1)}, s32[]{:T(128)}, /*index=5*/f32[1024,512]{1,0:T(8,128)S(1)}) %tuple.85), branch_computations={%region_1.1_spmd, %region_2.0_spmd} | conditional | flops 402784256 | bytes 1704070 | solution.py:51
  58.3 2.4 fusion
  63.2 6.8 %conditional.4 = (f32[2048,512]{1,0:T(8,128)}) conditional(s32[]{:T(128)} %convert_element_type.35, f32[2048,512]{1,0:T(8,128)} %get-tuple-element.475, (s32[32,2]{0,1:T(2,128)S(1)}, s32[]{:T(128)}, f32[2048,512]{1,0:T(8,128)}, bf16[32,256,256]{2,1,0:T(8,128)(2,1)}, s32[]{:T(128)}, /*index=5*/f32[1024,512]{1,0:T(8,128)S(1)}) %tuple.85), branch_computations={%region_1.1_spmd, %region_2.0_spmd} | conditional | flops 402784256 | bytes 1704070 | solution.py:51
  67.6 2.4 fusion
  72.6 6.8 %conditional.4 = (f32[2048,512]{1,0:T(8,128)}) conditional(s32[]{:T(128)} %convert_element_type.35, f32[2048,512]{1,0:T(8,128)} %get-tuple-element.475, (s32[32,2]{0,1:T(2,128)S(1)}, s32[]{:T(128)}, f32[2048,512]{1,0:T(8,128)}, bf16[32,256,256]{2,1,0:T(8,128)(2,1)}, s32[]{:T(128)}, /*index=5*/f32[1024,512]{1,0:T(8,128)S(1)}) %tuple.85), branch_computations={%region_1.1_spmd, %region_2.0_spmd} | conditional | flops 402784256 | bytes 1704070 | solution.py:51
  77.0 2.4 fusion
  154.0 7.7 %while.36 = (s32[]{:T(128)}, f32[2048,512]{1,0:T(8,128)}, s32[]{:T(128)}, s32[]{:T(128)}, f32[1024,512]{1,0:T(8,128)S(1)}, /*index=5*/s32[]{:T(128)}, s32[]{:T(128)}, s32[]{:T(128)}) while((s32[]{:T(128)}, f32[2048,512]{1,0:T(8,128)}, s32[]{:T(128)}, s32[]{:T(128)}, f32[1024,512]{1,0:T(8,128)S(1)}, /*index=5*/s32[]{:T(128)}, s32[]{:T(128)}, ...), condition=%wide.region_7.8_spmd, body=%wide.region_4.7_spmd.sunk | while | flops 131088 | bytes 1573139 | solution.py:69
  154.0 1.9 conditional.5
  154.0 1.9 add_dynamic-update-slice_fusion
  155.9 1.9 conditional.5
  155.9 1.9 add_dynamic-update-slice_fusion
  157.9 1.9 conditional.5
  157.9 1.9 add_dynamic-update-slice_fusion
  159.8 1.9 conditional.5
  159.8 1.9 add_dynamic-update-slice_fusion
  162.4 3.3 convert_reduce_fusion
  167.3 165.2 %all-reduce = f32[2048]{0:T(1024)S(1)} all-reduce(f32[2048]{0:T(1024)S(1)} %bitcast.23), channel_id=3, replica_groups=mesh['row'=4,'col'=8] {'col'}, use_global_device_ids=true, to_apply=%region_10.11.clone | all-reduce | flops 2048 | bytes 16384
  332.6 68.9 %reduce-scatter.2.cloned.1.call-done = f32[256,512]{1,0:T(8,128)} async-done(((f32[2048,512]{1,0:T(8,128)}), f32[256,512]{1,0:T(8,128)}) %reduce-scatter.2.cloned.1.call-update) | async-done | bytes 524304 | tf_op jit(solution)/shard_map/reduce_scatter | solution.py:72
  401.5 1.9 multiply_maximum_fusion
  (81 shorter events, 21.9 us)
Async XLA Ops:
  6.5 1.2 copy-start
  6.5 44.8 %copy-start.2 = (s32[1,1,32,2]{2,3,1,0:T(2,128)S(1)}, s32[1,1,32,2]{2,3,1,0:T(2,128)}, u32[]{:S(2)}) copy-start(s32[1,1,32,2]{2,3,1,0:T(2,128)} %param.16) | copy-start | bytes 772
  6.5 42.3 %all-gather.2.cloned.1.call-start = ((), (), s32[]{:S(2)}) async-start(), calls=%async_computation.1 | async-start | bytes 2621440 | tf_op jit(solution)/shard_map/all_gather | solution.py:33
  10.7 390.8 %reduce-scatter.2.cloned.1.call-start = ((), (), s32[]{:S(2)}) async-start(), calls=%async_computation.2 | async-start | bytes 4718592 | tf_op jit(solution)/shard_map/reduce_scatter | solution.py:72
  48.8 2.5 copy-start.1
  161.7 4.3 %copy-start.3 = (u32[32]{0:T(128)S(1)}, u32[32]{0:T(128)}, u32[]{:S(2)}) copy-start(u32[32]{0:T(128)} %constant.161) | copy-start | bytes 388
Sparse Core Ops, SparseCore 0:
  10.8 38.0 all-gather.1
  161.9 239.6 reduce-scatter.1
where the time goes:
time: 417 us; the launch traced here: 410 us
  blocking collectives  165 us (40%)
  waiting for transfers between devices  107 us (26%)
  loops' own time  75 us (18%)
  other arithmetic  33.6 us (8%)
  between operations  14.8 us (4%)
  matrix products  10.3 us (2%)
  local copies, waits for them, and re-layouts  4.31 us (1%)
    unnamed x1, blocking collectives  165 us
    reduce_scatter x1, waiting for transfers between devices, shards(): lax.psum_scatter(partial_value, 'col', scatter_dimension=0, tiled=True)  68.9 us
    another operation x1, loops' own time, shards(): partial_value = lax.fori_loop(0, slot_total, one_tile, partial_value)  63.2 us
    all_gather x1, waiting for transfers between devices, shards(): shard_rows = lax.all_gather(weighted, 'row', axis=0, tiled=True)  38.1 us
    mul x32, other arithmetic, one_tile(): col_offset = tile_slots[slot_index, 1] * tile_size  18.7 us
    another operation x32, loops' own time, one_tile(): return lax.cond(inside, add_tile, unchanged, current)  11.8 us
  transfers between devices with their start and end apart: 2, of which 2 were waited for; matrix products, arithmetic and copies ran while one was open for 1% of the time, Pallas kernels for 0%

commit v1 on v0

v1 whole, which is shorter than its diff:
```python
import functools

import jax
import jax.numpy as jnp
from jax import lax
from jax.experimental import pallas as pl
from jax.experimental.pallas import tpu as pltpu
from jax.sharding import PartitionSpec as P

LANES = 128
CORES = 2
GROUP = 8
QMAX = 32767.0
MESH = pl.DeviceIdType.MESH


def quantize(x, peak):
    inverse = QMAX / peak
    return jnp.round(x * inverse).astype(jnp.int32).astype(jnp.int16)


def row_peak(x):
    return jnp.maximum(jnp.max(jnp.abs(x), axis=1, keepdims=True), 1e-30)


def to_row(column):
    wide = jnp.broadcast_to(column, (LANES, LANES))
    eye = lax.broadcasted_iota(jnp.int32, (LANES, LANES), 0) == lax.broadcasted_iota(
        jnp.int32, (LANES, LANES), 1
    )
    return jnp.sum(jnp.where(eye, wide, 0.0), axis=0, keepdims=True)


def to_columns(row):
    return jnp.broadcast_to(row, (LANES, LANES)).T


def kernel(
    n_row, n_col, chunks, slots,
    feat_hbm, w_hbm, tiles_hbm, ids, count,
    out_ref,
    feat, weight, tiles, w_hi, w_lo,
    gq, gs, gscale, rhs, sums, degs,
    xs, xr, zq, zs, zr, zrs, own, ds, dr,
    last, prevs,
    in_sem, g_send, g_recv, gs_send, gs_recv, x_send, x_recv,
    z_send, z_recv, zs_send, zs_recv, d_send, d_recv,
):
    r = lax.axis_index("row")
    c = lax.axis_index("col")
    n_z = n_col // CORES
    z = c // CORES
    core = c % CORES
    other = 1 - core
    rows = feat.shape[0]
    halves = rows // LANES

    barrier = pltpu.get_barrier_semaphore()

    def greet_row(d, _):
        pl.semaphore_signal(barrier, inc=1, device_id=((r + d) % n_row, c), device_id_type=MESH)
        return 0

    def greet_col(d, _):
        pl.semaphore_signal(barrier, inc=1, device_id=(r, (c + d) % n_col), device_id_type=MESH)
        return 0

    lax.fori_loop(1, n_row, greet_row, 0)
    lax.fori_loop(1, n_col, greet_col, 0)

    load_f = pltpu.make_async_copy(feat_hbm, feat, in_sem.at[0])
    load_t = pltpu.make_async_copy(tiles_hbm, tiles, in_sem.at[1])
    load_w = pltpu.make_async_copy(w_hbm, weight, in_sem.at[2])
    load_f.start()
    load_t.start()
    load_w.start()

    for i in range(n_col):
        last[i] = 0

    def link(s, _):
        row = ids[s, 0]
        live = s < count[0, 0]
        prevs[s] = last[row]
        for i in range(n_col):
            last[i] = jnp.where(live & (row == i), s + 1, last[i])
        return 0

    load_f.wait()
    values = feat[...]
    peak = row_peak(values)
    for h in range(halves):
        gs[r, h : h + 1, :] = to_row(peak[h * LANES : (h + 1) * LANES] * (1.0 / QMAX))
    for k in range(chunks):
        gq[r, k] = quantize(values[:, k * LANES : (k + 1) * LANES], peak)

    pl.semaphore_wait(barrier, n_row + n_col - 2)

    def scale_copy(d, source):
        return pltpu.make_async_remote_copy(
            src_ref=gs.at[source], dst_ref=gs.at[source],
            send_sem=gs_send.at[d], recv_sem=gs_recv.at[d],
            device_id=((r + d) % n_row, c), device_id_type=MESH,
        )

    def gather_copy(k, d, source):
        return pltpu.make_async_remote_copy(
            src_ref=gq.at[source, k], dst_ref=gq.at[source, k],
            send_sem=g_send.at[k, d], recv_sem=g_recv.at[k, d],
            device_id=((r + d) % n_row, c), device_id_type=MESH,
        )

    def send_scale(d, _):
        scale_copy(d, r).start()
        return 0

    lax.fori_loop(1, n_row, send_scale, 0)

    def send_gather(t, _):
        gather_copy(t // (n_row - 1), t % (n_row - 1) + 1, r).start()
        return 0

    lax.fori_loop(0, chunks * (n_row - 1), send_gather, 0)

    lax.fori_loop(0, slots, link, 0)

    load_t.wait()
    degs[0] = jnp.zeros(degs.shape[1:], jnp.float32)
    sums[0] = jnp.zeros(sums.shape[1:], jnp.float32)

    def degree_slot(s, _):
        tile = tiles[s].astype(jnp.float32)
        part = degs[prevs[s]]
        for lane in range(0, tile.shape[1], LANES):
            part = part + tile[:, lane : lane + LANES]
        degs[s + 1] = part
        return 0

    lax.fori_loop(0, slots, degree_slot, 0)

    def degree_block(i, _):
        total = jnp.sum(degs[last[i]], axis=1, keepdims=True)
        for h in range(halves):
            ds[i, h : h + 1, :] = to_row(total[h * LANES : (h + 1) * LANES])
        return 0

    lax.fori_loop(0, n_col, degree_block, 0)

    def degree_copy(d):
        return pltpu.make_async_remote_copy(
            src_ref=ds.at[(c + d) % n_col], dst_ref=dr.at[d],
            send_sem=d_send.at[d], recv_sem=d_recv.at[d],
            device_id=(r, (c + d) % n_col), device_id_type=MESH,
        )

    def send_degree(d, _):
        degree_copy(d).start()
        return 0

    lax.fori_loop(1, n_col, send_degree, 0)

    load_w.wait()
    for k in range(chunks):
        part = weight[k * LANES : (k + 1) * LANES, :]
        high = part.astype(jnp.bfloat16)
        w_hi[k] = high
        w_lo[k] = (part - high.astype(jnp.float32)).astype(jnp.bfloat16)

    def wait_scale(d, _):
        scale_copy(d, (r + n_row - d) % n_row).wait_recv()
        return 0

    lax.fori_loop(1, n_row, wait_scale, 0)

    def spread_scale(j, _):
        for h in range(halves):
            gscale[j, h * LANES : (h + 1) * LANES, :] = to_columns(gs[j, h : h + 1, :])
        return 0

    lax.fori_loop(0, n_row, spread_scale, 0)

    def core_copy(k):
        return pltpu.make_async_remote_copy(
            src_ref=xs.at[k], dst_ref=xr.at[k],
            send_sem=x_send.at[k], recv_sem=x_recv.at[k],
            device_id=(r, z * CORES + other), device_id_type=MESH,
        )

    def z_copy(k, d):
        return pltpu.make_async_remote_copy(
            src_ref=zq.at[k, d], dst_ref=zr.at[k, d],
            send_sem=z_send.at[k, d], recv_sem=z_recv.at[k, d],
            device_id=(r, ((z + d) % n_z) * CORES + core), device_id_type=MESH,
        )

    def zs_copy(k, d):
        return pltpu.make_async_remote_copy(
            src_ref=zs.at[k, d], dst_ref=zrs.at[k, d],
            send_sem=zs_send.at[k, d], recv_sem=zs_recv.at[k, d],
            device_id=(r, ((z + d) % n_z) * CORES + core), device_id_type=MESH,
        )

    def local_block(i):
        j = r * n_col + i - c * n_row
        mine = (j >= 0) & (j < n_row)
        block = rhs[jnp.clip(j, 0, n_row - 1)].astype(jnp.float32)
        block = block[:, :LANES] + block[:, LANES:]
        return sums[last[i]] + jnp.where(mine, block, 0.0)

    def one_chunk(k, _):
        def wait_gather(d, _):
            gather_copy(k, d, (r + n_row - d) % n_row).wait_recv()
            return 0

        lax.fori_loop(1, n_row, wait_gather, 0)

        def decode(j, _):
            value = gq[j, k].astype(jnp.int32).astype(jnp.float32) * gscale[j]
            high = value.astype(jnp.bfloat16)
            rhs[j, :, :LANES] = high
            rhs[j, :, LANES:] = (value - high.astype(jnp.float32)).astype(jnp.bfloat16)
            return 0

        lax.fori_loop(0, n_row, decode, 0)

        def products(g, _):
            found = []
            for u in range(GROUP):
                s = g * GROUP + u
                both = jnp.dot(tiles[s], rhs[ids[s, 1]], preferred_element_type=jnp.float32)
                found.append(both[:, :LANES] + both[:, LANES:])
            for u in range(GROUP):
                s = g * GROUP + u
                sums[s + 1] = found[u] + sums[prevs[s]]
            return 0

        lax.fori_loop(0, slots // GROUP, products, 0)

        def hand_over(zz, _):
            xs[k, zz] = local_block(zz * CORES + other)
            return 0

        lax.fori_loop(0, n_z, hand_over, 0)
        core_copy(k).start()
        core_copy(k).wait_recv()

        def send_z(d, _):
            zz = (z + d) % n_z
            value = local_block(zz * CORES + core) + xr[k, zz]
            peak = row_peak(value)
            for h in range(halves):
                zs[k, d, h : h + 1, :] = to_row(peak[h * LANES : (h + 1) * LANES] * (1.0 / QMAX))
            zq[k, d] = quantize(value, peak)
            zs_copy(k, d).start()
            z_copy(k, d).start()
            return 0

        lax.fori_loop(1, n_z, send_z, 0)
        own[k] = local_block(z * CORES + core) + xr[k, z]
        return 0

    lax.fori_loop(0, chunks, one_chunk, 0)

    def add_degree(d, total):
        degree_copy(d).wait_recv()
        return total + dr[d]

    degree = lax.fori_loop(1, n_col, add_degree, 1.0 + ds[c])
    root = lax.rsqrt(degree)

    out_ref[...] = jnp.zeros(out_ref.shape, jnp.float32)

    def finish(k, _):
        def add_z(d, _):
            zs_copy(k, d).wait_recv()
            z_copy(k, d).wait_recv()
            for h in range(halves):
                part = slice(h * LANES, (h + 1) * LANES)
                scale = to_columns(zrs[k, d, h : h + 1, :])
                own[k, part] += zr[k, d, part].astype(jnp.int32).astype(jnp.float32) * scale
            return 0

        lax.fori_loop(1, n_z, add_z, 0)
        total = own[k]
        high = total.astype(jnp.bfloat16)
        low = (total - high.astype(jnp.float32)).astype(jnp.bfloat16)
        dot = functools.partial(jnp.dot, preferred_element_type=jnp.float32)
        out_ref[...] += dot(high, w_hi[k]) + (dot(high, w_lo[k]) + dot(low, w_hi[k]))
        return 0

    lax.fori_loop(0, chunks, finish, 0)
    for h in range(halves):
        part = slice(h * LANES, (h + 1) * LANES)
        factor = to_columns(root[h : h + 1, :])
        for k in range(chunks):
            cols = slice(k * LANES, (k + 1) * LANES)
            out_ref[part, cols] = jnp.maximum(out_ref[part, cols] * factor, 0.0)

    def drain_row(d, _):
        scale_copy(d, r).wait_send()

        def drain_chunk(k, _):
            gather_copy(k, d, r).wait_send()
            return 0

        lax.fori_loop(0, chunks, drain_chunk, 0)
        return 0

    def drain_degree(d, _):
        degree_copy(d).wait_send()
        return 0

    def drain_core(k, _):
        core_copy(k).wait_send()

        def drain_z(d, _):
            z_copy(k, d).wait_send()
            zs_copy(k, d).wait_send()
            return 0

        lax.fori_loop(1, n_z, drain_z, 0)
        return 0

    lax.fori_loop(1, n_row, drain_row, 0)
    lax.fori_loop(1, n_col, drain_degree, 0)
    lax.fori_loop(0, chunks, drain_core, 0)


def solution(mesh):
    n_row, n_col = mesh.shape["row"], mesh.shape["col"]
    n_z = n_col // CORES

    def shards(features, weight, tile_values, tile_ids, tile_counts):
        rows, width = features.shape
        slots, edge = tile_values.shape[2], tile_values.shape[3]
        chunks = width // LANES
        halves = rows // LANES
        f32, bf16, i16 = jnp.float32, jnp.bfloat16, jnp.int16
        dma = pltpu.SemaphoreType.DMA
        hbm = pl.BlockSpec(memory_space=pl.ANY)
        smem = pl.BlockSpec(memory_space=pltpu.SMEM)
        vmem = pl.BlockSpec(memory_space=pltpu.VMEM)
        return pl.pallas_call(
            functools.partial(kernel, n_row, n_col, chunks, slots),
            out_shape=jax.ShapeDtypeStruct((rows, width), f32),
            in_specs=[hbm, hbm, hbm, smem, smem],
            out_specs=vmem,
            scratch_shapes=[
                pltpu.VMEM((rows, width), f32),
                pltpu.VMEM((width, width), f32),
                pltpu.VMEM((slots, edge, edge), bf16),
                pltpu.VMEM((chunks, LANES, width), bf16),
                pltpu.VMEM((chunks, LANES, width), bf16),
                pltpu.VMEM((n_row, chunks, rows, LANES), i16),
                pltpu.VMEM((n_row, halves, LANES), f32),
                pltpu.VMEM((n_row, rows, LANES), f32),
                pltpu.VMEM((n_row, rows, 2 * LANES), bf16),
                pltpu.VMEM((slots + 1, edge, LANES), f32),
                pltpu.VMEM((slots + 1, edge, LANES), f32),
                pltpu.VMEM((chunks, n_z, rows, LANES), f32),
                pltpu.VMEM((chunks, n_z, rows, LANES), f32),
                pltpu.VMEM((chunks, n_z, rows, LANES), i16),
                pltpu.VMEM((chunks, n_z, halves, LANES), f32),
                pltpu.VMEM((chunks, n_z, rows, LANES), i16),
                pltpu.VMEM((chunks, n_z, halves, LANES), f32),
                pltpu.VMEM((chunks, rows, LANES), f32),
                pltpu.VMEM((n_col, halves, LANES), f32),
                pltpu.VMEM((n_col, halves, LANES), f32),
                pltpu.SMEM((n_col,), jnp.int32),
                pltpu.SMEM((slots,), jnp.int32),
                dma((3,)),
                dma((chunks, n_row)),
                dma((chunks, n_row)),
                dma((n_row,)),
                dma((n_row,)),
                dma((chunks,)),
                dma((chunks,)),
                dma((chunks, n_z)),
                dma((chunks, n_z)),
                dma((chunks, n_z)),
                dma((chunks, n_z)),
                dma((n_col,)),
                dma((n_col,)),
            ],
            compiler_params=pltpu.CompilerParams(
                collective_id=0, has_side_effects=True, vmem_limit_bytes=56 * 1024 * 1024
            ),
        )(
            features,
            weight,
            tile_values.reshape(slots, edge, edge),
            tile_ids.reshape(slots, 2),
            tile_counts,
        )

    in_specs = (
        P(("col", "row"), None),
        P(),
        P("row", "col", None, None, None),
        P("row", "col", None, None),
        P("row", "col"),
    )
    out_specs = P(("row", "col"), None)
    return jax.shard_map(shards, mesh=mesh, in_specs=in_specs, out_specs=out_specs, check_vma=False)
```

time: 417 us -> 45.2 us (0.11); the launches traced: 410 us -> 44.9 us
  blocking collectives: 165 us -> 0 us
  waiting for transfers between devices: 107 us -> 0 us
  loops' own time: 75 us -> 0 us
  Pallas kernels: 0 us -> 41 us
  other arithmetic: 33.6 us -> 0 us
  between operations: 14.8 us -> 0.66 us
  matrix products: 10.3 us -> 0 us
    unnamed x1 -> x0, blocking collectives: 165 us -> none
    another operation x38 -> x0, loops' own time: 75 us -> none  [the longest x1 63.2 us: shards(): partial_value = lax.fori_loop(0, slot_total, one_tile, partial_value)]
    reduce_scatter x1 -> x0, waiting for transfers between devices: 68.9 us -> none  [shards(): lax.psum_scatter(partial_value, 'col', scatter_dimension=0, tiled=True)]
    pallas_call x0 -> x1, Pallas kernels: none -> 41 us  [shards(): pl.pallas_call(functools.partial(kernel, n_row, n_col, chunks, slots), ou...]
    all_gather x1 -> x0, waiting for transfers between devices: 38.1 us -> none  [shards(): shard_rows = lax.all_gather(weighted, 'row', axis=0, tiled=True)]
    mul x35 -> x0, other arithmetic: 20.5 us -> none  [the longest x32 18.7 us: one_tile(): col_offset = tile_slots[slot_index, 1] * tile_size]
    dot_general x5 -> x0, matrix products: 10.3 us -> none  [the longest x3 7.2 us: add_tile(): jnp.dot(tile_set[slot_index].astype(jnp.float32), columns, precision=lax....]
    dynamic_update_slice x4 -> x0, other arithmetic: 7.67 us -> none  [add_self(): lax.dynamic_update_slice_in_dim(state, old_rows + own_block, row_blk * ti...]
  transfers between devices with their start and end apart: 2 -> 0, of which waited for: 2 -> 0; matrix products, arithmetic and copies ran while one was open for 1% -> 0% of each run, Pallas kernels for 0% -> 0%
where the time goes in v1:
time: 45.2 us; the launch traced here: 44.9 us
  Pallas kernels  41 us (91%)
  local copies, waits for them, and re-layouts  3.23 us (7%)
  between operations  0.66 us (1%)
    pallas_call x1, Pallas kernels, shards(): pl.pallas_call(functools.partial(kernel, n_row, n_col, chunks, slots), ou...  41 us
    unnamed x1, local copies, waits for them, and re-layouts  1.87 us
    reshape x1, local copies, waits for them, and re-layouts, shards(): tile_ids.reshape(slots, 2)  1.36 us

profile of v1, /device:TPU:0, one launch (start us, length us, event | category | flops | bytes accessed | tf_op | source)
XLA Modules:
  0.0 44.9 jit_solution(4139346996889254042)
XLA Ops:
  0.7 1.4 %copy.6.ids = s32[32,2]{1,0:T(8,128)} copy(s32[32,2]{0,1:T(2,128)} %bitcast.3) | data formatting | bytes 512 | tf_op jit(solution)/shard_map/reshape | solution.py:392
  2.0 41.0 %shard_map.55 = f32[256,512]{1,0:T(8,128)} custom-call(f32[256,512]{1,0:T(8,128)} %feat_hbm.1, f32[512,512]{1,0:T(8,128)} %w_hbm.1, bf16[32,256,256]{2,1,0:T(8,128)(2,1)} %bitcast.2, s32[32,2]{1,0:T(8,128)} %copy.6.ids, s32[1,1]{1,0:T(1,128)S(6)} %copy.8.count), custom_call_target="tpu_custom_call" | custom-call | tf_op jit(solution)/shard_map/pallas_call | solution.py:343
  43.0 1.9 %copy.9 = f32[256,512]{1,0:T(8,128)} copy(f32[256,512]{1,0:T(8,128)} %shard_map.55) | data formatting | bytes 1048576

commit v2 on v1

--- a/solution.py
+++ b/solution.py
@@ -41,7 +41,7 @@
     out_ref,
     feat, weight, tiles, w_hi, w_lo,
     gq, gs, gscale, rhs, sums, degs,
-    xs, xr, zq, zs, zr, zrs, own, ds, dr,
+    xs, xr, zq, zs, zr, zrs, ds, dr,
     last, prevs,
     in_sem, g_send, g_recv, gs_send, gs_recv, x_send, x_recv,
     z_send, z_recv, zs_send, zs_recv, d_send, d_recv,
@@ -79,7 +79,7 @@
         last[i] = 0
 
     def link(s, _):
-        row = ids[s, 0]
+        row = ids[0, s]
         live = s < count[0, 0]
         prevs[s] = last[row]
         for i in range(n_col):
@@ -116,11 +116,14 @@
 
     lax.fori_loop(1, n_row, send_scale, 0)
 
-    def send_gather(t, _):
-        gather_copy(t // (n_row - 1), t % (n_row - 1) + 1, r).start()
-        return 0
-
-    lax.fori_loop(0, chunks * (n_row - 1), send_gather, 0)
+    def send_gather(k):
+        def send(d, _):
+            gather_copy(k, d, r).start()
+            return 0
+
+        lax.fori_loop(1, n_row, send, 0)
+
+    send_gather(0)
 
     lax.fori_loop(0, slots, link, 0)
 
@@ -186,19 +189,74 @@
             device_id=(r, z * CORES + other), device_id_type=MESH,
         )
 
-    def z_copy(k, d):
-        return pltpu.make_async_remote_copy(
-            src_ref=zq.at[k, d], dst_ref=zr.at[k, d],
-            send_sem=z_send.at[k, d], recv_sem=z_recv.at[k, d],
-            device_id=(r, ((z + d) % n_z) * CORES + core), device_id_type=MESH,
-        )
-
-    def zs_copy(k, d):
-        return pltpu.make_async_remote_copy(
-            src_ref=zs.at[k, d], dst_ref=zrs.at[k, d],
-            send_sem=zs_send.at[k, d], recv_sem=zs_recv.at[k, d],
-            device_id=(r, ((z + d) % n_z) * CORES + core), device_id_type=MESH,
-        )
+    def z_copy(way, k, d):
+        step = 1 - 2 * way
+        target = jnp.clip(z + step, 0, n_z - 1) * CORES + core
+        at = way * chunks + k
+        return [
+            pltpu.make_async_remote_copy(
+                src_ref=source.at[at, d], dst_ref=landing.at[at, d],
+                send_sem=sent.at[at, d], recv_sem=landed.at[at, d],
+                device_id=(r, target), device_id_type=MESH,
+            )
+            for source, landing, sent, landed in (
+                (zs, zrs, zs_send, zs_recv), (zq, zr, z_send, z_recv),
+            )
+        ]
+
+    def received(way, k, d):
+        for copy in z_copy(way, k, d):
+            copy.wait_recv()
+        at = way * chunks + k
+        parts = []
+        for h in range(halves):
+            scale = to_columns(zrs[at, d, h : h + 1, :])
+            code = zr[at, d, h * LANES : (h + 1) * LANES]
+            parts.append(code.astype(jnp.int32).astype(jnp.float32) * scale)
+        return jnp.concatenate(parts, axis=0)
+
+    def hand_on(way, k, d, value):
+        at = way * chunks + k
+        peak = row_peak(value)
+        for h in range(halves):
+            zs[at, d, h : h + 1, :] = to_row(peak[h * LANES : (h + 1) * LANES] * (1.0 / QMAX))
+        zq[at, d] = quantize(value, peak)
+        for copy in z_copy(way, k, d):
+            copy.start()
+
+    top = n_z - 1
+
+    def begin(k):
+        def step(t, _):
+            @pl.when((z == 0) & (t < top))
+            def _():
+                hand_on(0, k, top - t, xr[k, top - t])
+
+            @pl.when((z == top) & (t < top))
+            def _():
+                hand_on(1, k, t, xr[k, t])
+
+            return 0
+
+        lax.fori_loop(0, top, step, 0)
+
+    def relay(k):
+        def step(t, _):
+            up = top - (t - z)
+
+            @pl.when((z > 0) & (t >= z) & (up > z))
+            def _():
+                hand_on(0, k, up, xr[k, up] + received(0, k, up))
+
+            down = t - (top - z)
+
+            @pl.when((z < top) & (down >= 0) & (down < z))
+            def _():
+                hand_on(1, k, down, xr[k, down] + received(1, k, down))
+
+            return 0
+
+        lax.fori_loop(1, top, step, 0)
 
     def local_block(i):
         j = r * n_col + i - c * n_row
@@ -214,6 +272,10 @@
 
         lax.fori_loop(1, n_row, wait_gather, 0)
 
+        @pl.when(k + 1 < chunks)
+        def _():
+            send_gather(k + 1)
+
         def decode(j, _):
             value = gq[j, k].astype(jnp.int32).astype(jnp.float32) * gscale[j]
             high = value.astype(jnp.bfloat16)
@@ -227,7 +289,7 @@
             found = []
             for u in range(GROUP):
                 s = g * GROUP + u
-                both = jnp.dot(tiles[s], rhs[ids[s, 1]], preferred_element_type=jnp.float32)
+                both = jnp.dot(tiles[s], rhs[ids[1, s]], preferred_element_type=jnp.float32)
                 found.append(both[:, :LANES] + both[:, LANES:])
             for u in range(GROUP):
                 s = g * GROUP + u
@@ -244,22 +306,21 @@
         core_copy(k).start()
         core_copy(k).wait_recv()
 
-        def send_z(d, _):
-            zz = (z + d) % n_z
-            value = local_block(zz * CORES + core) + xr[k, zz]
-            peak = row_peak(value)
-            for h in range(halves):
-                zs[k, d, h : h + 1, :] = to_row(peak[h * LANES : (h + 1) * LANES] * (1.0 / QMAX))
-            zq[k, d] = quantize(value, peak)
-            zs_copy(k, d).start()
-            z_copy(k, d).start()
-            return 0
-
-        lax.fori_loop(1, n_z, send_z, 0)
-        own[k] = local_block(z * CORES + core) + xr[k, z]
+        def add_own(zz, _):
+            xr[k, zz] += local_block(zz * CORES + core)
+            return 0
+
+        lax.fori_loop(0, n_z, add_own, 0)
+        begin(k)
+
+        @pl.when(k > 0)
+        def _():
+            relay(k - 1)
+
         return 0
 
     lax.fori_loop(0, chunks, one_chunk, 0)
+    relay(chunks - 1)
 
     def add_degree(d, total):
         degree_copy(d).wait_recv()
@@ -271,17 +332,15 @@
     out_ref[...] = jnp.zeros(out_ref.shape, jnp.float32)
 
     def finish(k, _):
-        def add_z(d, _):
-            zs_copy(k, d).wait_recv()
-            z_copy(k, d).wait_recv()
-            for h in range(halves):
-                part = slice(h * LANES, (h + 1) * LANES)
-                scale = to_columns(zrs[k, d, h : h + 1, :])
-                own[k, part] += zr[k, d, part].astype(jnp.int32).astype(jnp.float32) * scale
-            return 0
-
-        lax.fori_loop(1, n_z, add_z, 0)
-        total = own[k]
+        @pl.when(z > 0)
+        def _():
+            xr[k, z] += received(0, k, z)
+
+        @pl.when(z < top)
+        def _():
+            xr[k, z] += received(1, k, z)
+
+        total = xr[k, z]
         high = total.astype(jnp.bfloat16)
         low = (total - high.astype(jnp.float32)).astype(jnp.bfloat16)
         dot = functools.partial(jnp.dot, preferred_element_type=jnp.float32)
@@ -314,11 +373,19 @@
         core_copy(k).wait_send()
 
         def drain_z(d, _):
-            z_copy(k, d).wait_send()
-            zs_copy(k, d).wait_send()
-            return 0
-
-        lax.fori_loop(1, n_z, drain_z, 0)
+            @pl.when(d > z)
+            def _():
+                for copy in z_copy(0, k, d):
+                    copy.wait_send()
+
+            @pl.when(d < z)
+            def _():
+                for copy in z_copy(1, k, d):
+                    copy.wait_send()
+
+            return 0
+
+        lax.fori_loop(0, n_z, drain_z, 0)
         return 0
 
     lax.fori_loop(1, n_row, drain_row, 0)
@@ -359,11 +426,10 @@
                 pltpu.VMEM((slots + 1, edge, LANES), f32),
                 pltpu.VMEM((chunks, n_z, rows, LANES), f32),
                 pltpu.VMEM((chunks, n_z, rows, LANES), f32),
-                pltpu.VMEM((chunks, n_z, rows, LANES), i16),
-                pltpu.VMEM((chunks, n_z, halves, LANES), f32),
-                pltpu.VMEM((chunks, n_z, rows, LANES), i16),
-                pltpu.VMEM((chunks, n_z, halves, LANES), f32),
-                pltpu.VMEM((chunks, rows, LANES), f32),
+                pltpu.VMEM((2 * chunks, n_z, rows, LANES), i16),
+                pltpu.VMEM((2 * chunks, n_z, halves, LANES), f32),
+                pltpu.VMEM((2 * chunks, n_z, rows, LANES), i16),
+                pltpu.VMEM((2 * chunks, n_z, halves, LANES), f32),
                 pltpu.VMEM((n_col, halves, LANES), f32),
                 pltpu.VMEM((n_col, halves, LANES), f32),
                 pltpu.SMEM((n_col,), jnp.int32),
@@ -375,10 +441,10 @@
                 dma((n_row,)),
                 dma((chunks,)),
                 dma((chunks,)),
-                dma((chunks, n_z)),
-                dma((chunks, n_z)),
-                dma((chunks, n_z)),
-                dma((chunks, n_z)),
+                dma((2 * chunks, n_z)),
+                dma((2 * chunks, n_z)),
+                dma((2 * chunks, n_z)),
+                dma((2 * chunks, n_z)),
                 dma((n_col,)),
                 dma((n_col,)),
             ],
@@ -389,7 +455,7 @@
             features,
             weight,
             tile_values.reshape(slots, edge, edge),
-            tile_ids.reshape(slots, 2),
+            tile_ids.reshape(slots, 2).T,
             tile_counts,
         )
 

time: 45.2 us -> 54 us (1.19)
  Pallas kernels: 41 us -> 51.2 us
  local copies, waits for them, and re-layouts: 3.23 us -> 1.87 us
    pallas_call x1, Pallas kernels: 41 us -> 51.2 us  [shards(): pl.pallas_call(functools.partial(kernel, n_row, n_col, chunks, slots), ou...]
    reshape x1 -> x0, local copies, waits for them, and re-layouts: 1.36 us -> none  [shards(): tile_ids.reshape(slots, 2)]
where the time goes in v2:
time: 54 us; the launch traced here: 53.8 us
  Pallas kernels  51.2 us (95%)
  local copies, waits for them, and re-layouts  1.87 us (3%)
  between operations  0.66 us (1%)
    pallas_call x1, Pallas kernels, shards(): pl.pallas_call(functools.partial(kernel, n_row, n_col, chunks, slots), ou...  51.2 us
    unnamed x1, local copies, waits for them, and re-layouts  1.87 us

profile of v2, /device:TPU:0, one launch (start us, length us, event | category | flops | bytes accessed | tf_op | source)
XLA Modules:
  0.0 53.8 jit_solution(11408243027346606377)
XLA Ops:
  0.7 51.2 %shard_map.55 = f32[256,512]{1,0:T(8,128)} custom-call(f32[256,512]{1,0:T(8,128)} %feat_hbm.1, f32[512,512]{1,0:T(8,128)} %w_hbm.1, bf16[32,256,256]{2,1,0:T(8,128)(2,1)} %bitcast.4, s32[2,32]{1,0:T(2,128)} %bitcast.5, s32[1,1]{1,0:T(1,128)S(6)} %copy.7.count), custom_call_target="tpu_custom_call" | custom-call | tf_op jit(solution)/shard_map/pallas_call | solution.py:410
  51.9 1.9 %copy.8 = f32[256,512]{1,0:T(8,128)} copy(f32[256,512]{1,0:T(8,128)} %shard_map.55) | data formatting | bytes 1048576

commit v3 on v1

--- a/solution.py
+++ b/solution.py
@@ -41,7 +41,7 @@
     out_ref,
     feat, weight, tiles, w_hi, w_lo,
     gq, gs, gscale, rhs, sums, degs,
-    xs, xr, zq, zs, zr, zrs, own, ds, dr,
+    xs, xr, zq, zs, zr, zrs, own, mine, ds, dr,
     last, prevs,
     in_sem, g_send, g_recv, gs_send, gs_recv, x_send, x_recv,
     z_send, z_recv, zs_send, zs_recv, d_send, d_recv,
@@ -79,7 +79,7 @@
         last[i] = 0
 
     def link(s, _):
-        row = ids[s, 0]
+        row = ids[0, s]
         live = s < count[0, 0]
         prevs[s] = last[row]
         for i in range(n_col):
@@ -116,35 +116,19 @@
 
     lax.fori_loop(1, n_row, send_scale, 0)
 
-    def send_gather(t, _):
-        gather_copy(t // (n_row - 1), t % (n_row - 1) + 1, r).start()
-        return 0
-
-    lax.fori_loop(0, chunks * (n_row - 1), send_gather, 0)
+    def send_gather(k):
+        def send(d, _):
+            gather_copy(k, d, r).start()
+            return 0
+
+        lax.fori_loop(1, n_row, send, 0)
+
+    send_gather(0)
 
     lax.fori_loop(0, slots, link, 0)
 
     load_t.wait()
-    degs[0] = jnp.zeros(degs.shape[1:], jnp.float32)
     sums[0] = jnp.zeros(sums.shape[1:], jnp.float32)
-
-    def degree_slot(s, _):
-        tile = tiles[s].astype(jnp.float32)
-        part = degs[prevs[s]]
-        for lane in range(0, tile.shape[1], LANES):
-            part = part + tile[:, lane : lane + LANES]
-        degs[s + 1] = part
-        return 0
-
-    lax.fori_loop(0, slots, degree_slot, 0)
-
-    def degree_block(i, _):
-        total = jnp.sum(degs[last[i]], axis=1, keepdims=True)
-        for h in range(halves):
-            ds[i, h : h + 1, :] = to_row(total[h * LANES : (h + 1) * LANES])
-        return 0
-
-    lax.fori_loop(0, n_col, degree_block, 0)
 
     def degree_copy(d):
         return pltpu.make_async_remote_copy(
@@ -153,36 +137,10 @@
             device_id=(r, (c + d) % n_col), device_id_type=MESH,
         )
 
-    def send_degree(d, _):
-        degree_copy(d).start()
-        return 0
-
-    lax.fori_loop(1, n_col, send_degree, 0)
-
-    load_w.wait()
-    for k in range(chunks):
-        part = weight[k * LANES : (k + 1) * LANES, :]
-        high = part.astype(jnp.bfloat16)
-        w_hi[k] = high
-        w_lo[k] = (part - high.astype(jnp.float32)).astype(jnp.bfloat16)
-
-    def wait_scale(d, _):
-        scale_copy(d, (r + n_row - d) % n_row).wait_recv()
-        return 0
-
-    lax.fori_loop(1, n_row, wait_scale, 0)
-
-    def spread_scale(j, _):
-        for h in range(halves):
-            gscale[j, h * LANES : (h + 1) * LANES, :] = to_columns(gs[j, h : h + 1, :])
-        return 0
-
-    lax.fori_loop(0, n_row, spread_scale, 0)
-
-    def core_copy(k):
-        return pltpu.make_async_remote_copy(
-            src_ref=xs.at[k], dst_ref=xr.at[k],
-            send_sem=x_send.at[k], recv_sem=x_recv.at[k],
+    def core_copy(k, d):
+        return pltpu.make_async_remote_copy(
+            src_ref=xs.at[k, d], dst_ref=xr.at[k, d],
+            send_sem=x_send.at[k, d], recv_sem=x_recv.at[k, d],
             device_id=(r, z * CORES + other), device_id_type=MESH,
         )
 
@@ -202,10 +160,67 @@
 
     def local_block(i):
         j = r * n_col + i - c * n_row
-        mine = (j >= 0) & (j < n_row)
+        inside = (j >= 0) & (j < n_row)
         block = rhs[jnp.clip(j, 0, n_row - 1)].astype(jnp.float32)
         block = block[:, :LANES] + block[:, LANES:]
-        return sums[last[i]] + jnp.where(mine, block, 0.0)
+        return sums[last[i]] + jnp.where(inside, block, 0.0)
+
+    def row_sums():
+        degs[0] = jnp.zeros(degs.shape[1:], jnp.float32)
+
+        def degree_slot(s, _):
+            tile = tiles[s].astype(jnp.float32)
+            part = degs[prevs[s]]
+            for lane in range(0, tile.shape[1], LANES):
+                part = part + tile[:, lane : lane + LANES]
+            degs[s + 1] = part
+            return 0
+
+        lax.fori_loop(0, slots, degree_slot, 0)
+
+        def degree_block(i, _):
+            total = jnp.sum(degs[last[i]], axis=1, keepdims=True)
+            for h in range(halves):
+                ds[i, h : h + 1, :] = to_row(total[h * LANES : (h + 1) * LANES])
+            return 0
+
+        lax.fori_loop(0, n_col, degree_block, 0)
+
+        def send_degree(d, _):
+            degree_copy(d).start()
+            return 0
+
+        lax.fori_loop(1, n_col, send_degree, 0)
+
+    def split_weight():
+        load_w.wait()
+        for k in range(chunks):
+            part = weight[k * LANES : (k + 1) * LANES, :]
+            high = part.astype(jnp.bfloat16)
+            w_hi[k] = high
+            w_lo[k] = (part - high.astype(jnp.float32)).astype(jnp.bfloat16)
+
+    def received(k, d):
+        zs_copy(k, d).wait_recv()
+        z_copy(k, d).wait_recv()
+        parts = []
+        for h in range(halves):
+            code = zr[k, d, h * LANES : (h + 1) * LANES]
+            scale = to_columns(zrs[k, d, h : h + 1, :])
+            parts.append(code.astype(jnp.int32).astype(jnp.float32) * scale)
+        return jnp.concatenate(parts, axis=0)
+
+    def project(k):
+        def add_z(d, _):
+            own[k] += received(k, d)
+            return 0
+
+        lax.fori_loop(1, n_z, add_z, 0)
+        total = own[k]
+        high = total.astype(jnp.bfloat16)
+        low = (total - high.astype(jnp.float32)).astype(jnp.bfloat16)
+        dot = functools.partial(jnp.dot, preferred_element_type=jnp.float32)
+        out_ref[...] += dot(high, w_hi[k]) + (dot(high, w_lo[k]) + dot(low, w_hi[k]))
 
     def one_chunk(k, _):
         def wait_gather(d, _):
@@ -213,6 +228,10 @@
             return 0
 
         lax.fori_loop(1, n_row, wait_gather, 0)
+
+        @pl.when(k + 1 < chunks)
+        def _():
+            send_gather(k + 1)
 
         def decode(j, _):
             value = gq[j, k].astype(jnp.int32).astype(jnp.float32) * gscale[j]
@@ -224,29 +243,39 @@
         lax.fori_loop(0, n_row, decode, 0)
 
         def products(g, _):
-            found = []
             for u in range(GROUP):
                 s = g * GROUP + u
-                both = jnp.dot(tiles[s], rhs[ids[s, 1]], preferred_element_type=jnp.float32)
-                found.append(both[:, :LANES] + both[:, LANES:])
-            for u in range(GROUP):
-                s = g * GROUP + u
-                sums[s + 1] = found[u] + sums[prevs[s]]
+                both = jnp.dot(tiles[s], rhs[ids[1, s]], preferred_element_type=jnp.float32)
+                sums[s + 1] = both[:, :LANES] + both[:, LANES:] + sums[prevs[s]]
             return 0
 
         lax.fori_loop(0, slots // GROUP, products, 0)
 
-        def hand_over(zz, _):
-            xs[k, zz] = local_block(zz * CORES + other)
-            return 0
-
-        lax.fori_loop(0, n_z, hand_over, 0)
-        core_copy(k).start()
-        core_copy(k).wait_recv()
+        def hand_over(d, _):
+            zz = (z + d) % n_z
+            xs[k, d] = local_block(zz * CORES + other)
+            core_copy(k, d).start()
+            return 0
+
+        lax.fori_loop(1, n_z + 1, hand_over, 0)
+
+        def keep(d, _):
+            mine[d] = local_block((z + d) % n_z * CORES + core)
+            return 0
+
+        lax.fori_loop(1, n_z + 1, keep, 0)
+
+        @pl.when(k == 0)
+        def _():
+            split_weight()
+
+        @pl.when(k >= 2)
+        def _():
+            project(k - 2)
 
         def send_z(d, _):
-            zz = (z + d) % n_z
-            value = local_block(zz * CORES + core) + xr[k, zz]
+            core_copy(k, d).wait_recv()
+            value = mine[d] + xr[k, d]
             peak = row_peak(value)
             for h in range(halves):
                 zs[k, d, h : h + 1, :] = to_row(peak[h * LANES : (h + 1) * LANES] * (1.0 / QMAX))
@@ -256,9 +285,25 @@
             return 0
 
         lax.fori_loop(1, n_z, send_z, 0)
-        own[k] = local_block(z * CORES + core) + xr[k, z]
-        return 0
-
+        core_copy(k, n_z).wait_recv()
+        own[k] = mine[n_z] + xr[k, n_z]
+        return 0
+
+    row_sums()
+
+    def wait_scale(d, _):
+        scale_copy(d, (r + n_row - d) % n_row).wait_recv()
+        return 0
+
+    lax.fori_loop(1, n_row, wait_scale, 0)
+
+    def spread_scale(j, _):
+        for h in range(halves):
+            gscale[j, h * LANES : (h + 1) * LANES, :] = to_columns(gs[j, h : h + 1, :])
+        return 0
+
+    lax.fori_loop(0, n_row, spread_scale, 0)
+    out_ref[...] = jnp.zeros(out_ref.shape, jnp.float32)
     lax.fori_loop(0, chunks, one_chunk, 0)
 
     def add_degree(d, total):
@@ -268,27 +313,8 @@
     degree = lax.fori_loop(1, n_col, add_degree, 1.0 + ds[c])
     root = lax.rsqrt(degree)
 
-    out_ref[...] = jnp.zeros(out_ref.shape, jnp.float32)
-
-    def finish(k, _):
-        def add_z(d, _):
-            zs_copy(k, d).wait_recv()
-            z_copy(k, d).wait_recv()
-            for h in range(halves):
-                part = slice(h * LANES, (h + 1) * LANES)
-                scale = to_columns(zrs[k, d, h : h + 1, :])
-                own[k, part] += zr[k, d, part].astype(jnp.int32).astype(jnp.float32) * scale
-            return 0
-
-        lax.fori_loop(1, n_z, add_z, 0)
-        total = own[k]
-        high = total.astype(jnp.bfloat16)
-        low = (total - high.astype(jnp.float32)).astype(jnp.bfloat16)
-        dot = functools.partial(jnp.dot, preferred_element_type=jnp.float32)
-        out_ref[...] += dot(high, w_hi[k]) + (dot(high, w_lo[k]) + dot(low, w_hi[k]))
-        return 0
-
-    lax.fori_loop(0, chunks, finish, 0)
+    for k in range(max(chunks - 2, 0), chunks):
+        project(k)
     for h in range(halves):
         part = slice(h * LANES, (h + 1) * LANES)
         factor = to_columns(root[h : h + 1, :])
@@ -311,7 +337,11 @@
         return 0
 
     def drain_core(k, _):
-        core_copy(k).wait_send()
+        def drain_x(d, _):
+            core_copy(k, d).wait_send()
+            return 0
+
+        lax.fori_loop(1, n_z + 1, drain_x, 0)
 
         def drain_z(d, _):
             z_copy(k, d).wait_send()
@@ -357,13 +387,14 @@
                 pltpu.VMEM((n_row, rows, 2 * LANES), bf16),
                 pltpu.VMEM((slots + 1, edge, LANES), f32),
                 pltpu.VMEM((slots + 1, edge, LANES), f32),
-                pltpu.VMEM((chunks, n_z, rows, LANES), f32),
-                pltpu.VMEM((chunks, n_z, rows, LANES), f32),
+                pltpu.VMEM((chunks, n_z + 1, rows, LANES), f32),
+                pltpu.VMEM((chunks, n_z + 1, rows, LANES), f32),
                 pltpu.VMEM((chunks, n_z, rows, LANES), i16),
                 pltpu.VMEM((chunks, n_z, halves, LANES), f32),
                 pltpu.VMEM((chunks, n_z, rows, LANES), i16),
                 pltpu.VMEM((chunks, n_z, halves, LANES), f32),
                 pltpu.VMEM((chunks, rows, LANES), f32),
+                pltpu.VMEM((n_z + 1, rows, LANES), f32),
                 pltpu.VMEM((n_col, halves, LANES), f32),
                 pltpu.VMEM((n_col, halves, LANES), f32),
                 pltpu.SMEM((n_col,), jnp.int32),
@@ -373,8 +404,8 @@
                 dma((chunks, n_row)),
                 dma((n_row,)),
                 dma((n_row,)),
-                dma((chunks,)),
-                dma((chunks,)),
+                dma((chunks, n_z + 1)),
+                dma((chunks, n_z + 1)),
                 dma((chunks, n_z)),
                 dma((chunks, n_z)),
                 dma((chunks, n_z)),
@@ -389,7 +420,7 @@
             features,
             weight,
             tile_values.reshape(slots, edge, edge),
-            tile_ids.reshape(slots, 2),
+            tile_ids.reshape(slots, 2).T,
             tile_counts,
         )
 

time: 45.2 us -> 43.3 us (0.958)
  local copies, waits for them, and re-layouts: 3.23 us -> 1.87 us
    reshape x1 -> x0, local copies, waits for them, and re-layouts: 1.36 us -> none  [shards(): tile_ids.reshape(slots, 2)]
where the time goes in v3:
time: 43.3 us; the launch traced here: 43.1 us
  Pallas kernels  40.6 us (94%)
  local copies, waits for them, and re-layouts  1.87 us (4%)
  between operations  0.66 us (2%)
    pallas_call x1, Pallas kernels, shards(): pl.pallas_call(functools.partial(kernel, n_row, n_col, chunks, slots), ou...  40.6 us
    unnamed x1, local copies, waits for them, and re-layouts  1.87 us

profile of v3, /device:TPU:0, one launch (start us, length us, event | category | flops | bytes accessed | tf_op | source)
XLA Modules:
  0.0 43.1 jit_solution(10635572333102748602)
XLA Ops:
  0.7 40.6 %shard_map.55 = f32[256,512]{1,0:T(8,128)} custom-call(f32[256,512]{1,0:T(8,128)} %feat_hbm.1, f32[512,512]{1,0:T(8,128)} %w_hbm.1, bf16[32,256,256]{2,1,0:T(8,128)(2,1)} %bitcast.4, s32[2,32]{1,0:T(2,128)} %bitcast.5, s32[1,1]{1,0:T(1,128)S(6)} %copy.7.count), custom_call_target="tpu_custom_call" | custom-call | tf_op jit(solution)/shard_map/pallas_call | solution.py:373
  41.3 1.9 %copy.8 = f32[256,512]{1,0:T(8,128)} copy(f32[256,512]{1,0:T(8,128)} %shard_map.55) | data formatting | bytes 1048576

commit v4 on v3

--- a/solution.py
+++ b/solution.py
@@ -9,7 +9,7 @@
 
 LANES = 128
 CORES = 2
-GROUP = 8
+GROUP = 32
 QMAX = 32767.0
 MESH = pl.DeviceIdType.MESH
 
@@ -144,19 +144,43 @@
             device_id=(r, z * CORES + other), device_id_type=MESH,
         )
 
-    def z_copy(k, d):
-        return pltpu.make_async_remote_copy(
-            src_ref=zq.at[k, d], dst_ref=zr.at[k, d],
-            send_sem=z_send.at[k, d], recv_sem=z_recv.at[k, d],
-            device_id=(r, ((z + d) % n_z) * CORES + core), device_id_type=MESH,
-        )
-
-    def zs_copy(k, d):
-        return pltpu.make_async_remote_copy(
-            src_ref=zs.at[k, d], dst_ref=zrs.at[k, d],
-            send_sem=zs_send.at[k, d], recv_sem=zs_recv.at[k, d],
-            device_id=(r, ((z + d) % n_z) * CORES + core), device_id_type=MESH,
-        )
+    def z_copies(k, d, target):
+        return [
+            pltpu.make_async_remote_copy(
+                src_ref=source.at[k, d], dst_ref=landing.at[k, d],
+                send_sem=sent.at[k, d], recv_sem=landed.at[k, d],
+                device_id=(r, target * CORES + core), device_id_type=MESH,
+            )
+            for source, landing, sent, landed in (
+                (zs, zrs, zs_send, zs_recv), (zq, zr, z_send, z_recv),
+            )
+        ]
+
+    top = n_z - 1
+    relays = n_z > 2
+
+    def transmit(k, d, target, value):
+        peak = row_peak(value)
+        for h in range(halves):
+            zs[k, d, h : h + 1, :] = to_row(peak[h * LANES : (h + 1) * LANES] * (1.0 / QMAX))
+        zq[k, d] = quantize(value, peak)
+        for copy in z_copies(k, d, target):
+            copy.start()
+
+    def distance(t):
+        return jnp.where((z == top) | (t == n_z), t, n_z - t)
+
+    def relay(k):
+        if not relays:
+            return
+
+        @pl.when(z == 1)
+        def _():
+            transmit(k, top - 1, top, xr[k, top - 1] + received(k, n_z))
+
+        @pl.when(z == top - 1)
+        def _():
+            transmit(k, 2, 0, xr[k, 2] + received(k, n_z + 1))
 
     def local_block(i):
         j = r * n_col + i - c * n_row
@@ -201,8 +225,8 @@
             w_lo[k] = (part - high.astype(jnp.float32)).astype(jnp.bfloat16)
 
     def received(k, d):
-        zs_copy(k, d).wait_recv()
-        z_copy(k, d).wait_recv()
+        for copy in z_copies(k, d, jnp.where(z == 0, 1, 0)):
+            copy.wait_recv()
         parts = []
         for h in range(halves):
             code = zr[k, d, h * LANES : (h + 1) * LANES]
@@ -212,7 +236,13 @@
 
     def project(k):
         def add_z(d, _):
-            own[k] += received(k, d)
+            source = (z + n_z - d) % n_z
+            far = ((z == 0) & (source == top)) | ((z == top) & (source == 0))
+
+            @pl.when(jnp.logical_not(far & relays))
+            def _():
+                own[k] += received(k, d)
+
             return 0
 
         lax.fori_loop(1, n_z, add_z, 0)
@@ -251,7 +281,8 @@
 
         lax.fori_loop(0, slots // GROUP, products, 0)
 
-        def hand_over(d, _):
+        def hand_over(t, _):
+            d = distance(t)
             zz = (z + d) % n_z
             xs[k, d] = local_block(zz * CORES + other)
             core_copy(k, d).start()
@@ -269,19 +300,33 @@
         def _():
             split_weight()
 
+        @pl.when(k >= 1)
+        def _():
+            relay(k - 1)
+
         @pl.when(k >= 2)
         def _():
             project(k - 2)
 
-        def send_z(d, _):
+        def send_z(t, _):
+            d = distance(t)
+            zz = (z + d) % n_z
             core_copy(k, d).wait_recv()
             value = mine[d] + xr[k, d]
-            peak = row_peak(value)
-            for h in range(halves):
-                zs[k, d, h : h + 1, :] = to_row(peak[h * LANES : (h + 1) * LANES] * (1.0 / QMAX))
-            zq[k, d] = quantize(value, peak)
-            zs_copy(k, d).start()
-            z_copy(k, d).start()
+            from_low = (z == 0) & (zz == top) & relays
+            from_high = (z == top) & (zz == 0) & relays
+            held = (((z == 1) & (zz == top)) | ((z == top - 1) & (zz == 0))) & relays
+
+            @pl.when(held)
+            def _():
+                xr[k, d] = value
+
+            @pl.when(jnp.logical_not(held))
+            def _():
+                slot = jnp.where(from_low, n_z, jnp.where(from_high, n_z + 1, d))
+                target = jnp.where(from_low, 1, jnp.where(from_high, top - 1, zz))
+                transmit(k, slot, target, value)
+
             return 0
 
         lax.fori_loop(1, n_z, send_z, 0)
@@ -313,6 +358,7 @@
     degree = lax.fori_loop(1, n_col, add_degree, 1.0 + ds[c])
     root = lax.rsqrt(degree)
 
+    relay(chunks - 1)
     for k in range(max(chunks - 2, 0), chunks):
         project(k)
     for h in range(halves):
@@ -344,8 +390,12 @@
         lax.fori_loop(1, n_z + 1, drain_x, 0)
 
         def drain_z(d, _):
-            z_copy(k, d).wait_send()
-            zs_copy(k, d).wait_send()
+            target = (z + d) % n_z
+            from_low = (z == 0) & (target == top) & relays
+            from_high = (z == top) & (target == 0) & relays
+            slot = jnp.where(from_low, n_z, jnp.where(from_high, n_z + 1, d))
+            for copy in z_copies(k, slot, target):
+                copy.wait_send()
             return 0
 
         lax.fori_loop(1, n_z, drain_z, 0)
@@ -389,10 +439,10 @@
                 pltpu.VMEM((slots + 1, edge, LANES), f32),
                 pltpu.VMEM((chunks, n_z + 1, rows, LANES), f32),
                 pltpu.VMEM((chunks, n_z + 1, rows, LANES), f32),
-                pltpu.VMEM((chunks, n_z, rows, LANES), i16),
-                pltpu.VMEM((chunks, n_z, halves, LANES), f32),
-                pltpu.VMEM((chunks, n_z, rows, LANES), i16),
-                pltpu.VMEM((chunks, n_z, halves, LANES), f32),
+                pltpu.VMEM((chunks, n_z + 2, rows, LANES), i16),
+                pltpu.VMEM((chunks, n_z + 2, halves, LANES), f32),
+                pltpu.VMEM((chunks, n_z + 2, rows, LANES), i16),
+                pltpu.VMEM((chunks, n_z + 2, halves, LANES), f32),
                 pltpu.VMEM((chunks, rows, LANES), f32),
                 pltpu.VMEM((n_z + 1, rows, LANES), f32),
                 pltpu.VMEM((n_col, halves, LANES), f32),
@@ -406,10 +456,10 @@
                 dma((n_row,)),
                 dma((chunks, n_z + 1)),
                 dma((chunks, n_z + 1)),
-                dma((chunks, n_z)),
-                dma((chunks, n_z)),
-                dma((chunks, n_z)),
-                dma((chunks, n_z)),
+                dma((chunks, n_z + 2)),
+                dma((chunks, n_z + 2)),
+                dma((chunks, n_z + 2)),
+                dma((chunks, n_z + 2)),
                 dma((n_col,)),
                 dma((n_col,)),
             ],

time: 43.3 us -> 41.3 us (0.954)
  Pallas kernels: 40.6 us -> 38.6 us
    pallas_call x1, Pallas kernels: 40.6 us -> 38.6 us  [shards(): pl.pallas_call(functools.partial(kernel, n_row, n_col, chunks, slots), ou...]
where the time goes in v4:
time: 41.3 us; the launch traced here: 41.1 us
  Pallas kernels  38.6 us (93%)
  local copies, waits for them, and re-layouts  1.87 us (5%)
  between operations  0.66 us (2%)
    pallas_call x1, Pallas kernels, shards(): pl.pallas_call(functools.partial(kernel, n_row, n_col, chunks, slots), ou...  38.6 us
    unnamed x1, local copies, waits for them, and re-layouts  1.87 us

profile of v4, /device:TPU:0, one launch (start us, length us, event | category | flops | bytes accessed | tf_op | source)
XLA Modules:
  0.0 41.1 jit_solution(17911745142308111929)
XLA Ops:
  0.7 38.6 %shard_map.55 = f32[256,512]{1,0:T(8,128)} custom-call(f32[256,512]{1,0:T(8,128)} %feat_hbm.1, f32[512,512]{1,0:T(8,128)} %w_hbm.1, bf16[32,256,256]{2,1,0:T(8,128)(2,1)} %bitcast.4, s32[2,32]{1,0:T(2,128)} %bitcast.5, s32[1,1]{1,0:T(1,128)S(6)} %copy.7.count), custom_call_target="tpu_custom_call" | custom-call | tf_op jit(solution)/shard_map/pallas_call | solution.py:423
  39.3 1.9 %copy.8 = f32[256,512]{1,0:T(8,128)} copy(f32[256,512]{1,0:T(8,128)} %shard_map.55) | data formatting | bytes 1048576

commit v5 on v4

--- a/solution.py
+++ b/solution.py
@@ -41,7 +41,7 @@
     out_ref,
     feat, weight, tiles, w_hi, w_lo,
     gq, gs, gscale, rhs, sums, degs,
-    xs, xr, zq, zs, zr, zrs, own, mine, ds, dr,
+    xs, xr, zq, zs, zr, zrs, own, kept, ds, dr,
     last, prevs,
     in_sem, g_send, g_recv, gs_send, gs_recv, x_send, x_recv,
     z_send, z_recv, zs_send, zs_recv, d_send, d_recv,
@@ -76,14 +76,14 @@
     load_w.start()
 
     for i in range(n_col):
-        last[i] = 0
+        last[i] = i
 
     def link(s, _):
         row = ids[0, s]
         live = s < count[0, 0]
         prevs[s] = last[row]
         for i in range(n_col):
-            last[i] = jnp.where(live & (row == i), s + 1, last[i])
+            last[i] = jnp.where(live & (row == i), n_col + s, last[i])
         return 0
 
     load_f.wait()
@@ -128,7 +128,6 @@
     lax.fori_loop(0, slots, link, 0)
 
     load_t.wait()
-    sums[0] = jnp.zeros(sums.shape[1:], jnp.float32)
 
     def degree_copy(d):
         return pltpu.make_async_remote_copy(
@@ -159,11 +158,14 @@
     top = n_z - 1
     relays = n_z > 2
 
-    def transmit(k, d, target, value):
+    def encode(k, d, value):
         peak = row_peak(value)
         for h in range(halves):
             zs[k, d, h : h + 1, :] = to_row(peak[h * LANES : (h + 1) * LANES] * (1.0 / QMAX))
         zq[k, d] = quantize(value, peak)
+
+    def transmit(k, d, target, value):
+        encode(k, d, value)
         for copy in z_copies(k, d, target):
             copy.start()
 
@@ -176,31 +178,26 @@
 
         @pl.when(z == 1)
         def _():
-            transmit(k, top - 1, top, xr[k, top - 1] + received(k, n_z))
+            transmit(k, top - 1, top, kept[k, top - 1] + received(k, n_z))
 
         @pl.when(z == top - 1)
         def _():
-            transmit(k, 2, 0, xr[k, 2] + received(k, n_z + 1))
-
-    def local_block(i):
-        j = r * n_col + i - c * n_row
-        inside = (j >= 0) & (j < n_row)
-        block = rhs[jnp.clip(j, 0, n_row - 1)].astype(jnp.float32)
-        block = block[:, :LANES] + block[:, LANES:]
-        return sums[last[i]] + jnp.where(inside, block, 0.0)
+            transmit(k, 2, 0, kept[k, 2] + received(k, n_z + 1))
 
     def row_sums():
-        degs[0] = jnp.zeros(degs.shape[1:], jnp.float32)
+        for i in range(n_col):
+            degs[i] = jnp.zeros(degs.shape[1:], jnp.float32)
+            sums[i] = jnp.zeros(sums.shape[1:], jnp.float32)
 
         def degree_slot(s, _):
             tile = tiles[s].astype(jnp.float32)
             part = degs[prevs[s]]
             for lane in range(0, tile.shape[1], LANES):
                 part = part + tile[:, lane : lane + LANES]
-            degs[s + 1] = part
-            return 0
-
-        lax.fori_loop(0, slots, degree_slot, 0)
+            degs[n_col + s] = part
+            return 0
+
+        lax.fori_loop(0, slots, degree_slot, 0, unroll=8)
 
         def degree_block(i, _):
             total = jnp.sum(degs[last[i]], axis=1, keepdims=True)
@@ -208,7 +205,7 @@
                 ds[i, h : h + 1, :] = to_row(total[h * LANES : (h + 1) * LANES])
             return 0
 
-        lax.fori_loop(0, n_col, degree_block, 0)
+        lax.fori_loop(0, n_col, degree_block, 0, unroll=8)
 
         def send_degree(d, _):
             degree_copy(d).start()
@@ -224,9 +221,11 @@
             w_hi[k] = high
             w_lo[k] = (part - high.astype(jnp.float32)).astype(jnp.bfloat16)
 
-    def received(k, d):
+    def arrive(k, d):
         for copy in z_copies(k, d, jnp.where(z == 0, 1, 0)):
             copy.wait_recv()
+
+    def decoded(k, d):
         parts = []
         for h in range(halves):
             code = zr[k, d, h * LANES : (h + 1) * LANES]
@@ -234,19 +233,28 @@
             parts.append(code.astype(jnp.int32).astype(jnp.float32) * scale)
         return jnp.concatenate(parts, axis=0)
 
+    def received(k, d):
+        arrive(k, d)
+        return decoded(k, d)
+
     def project(k):
-        def add_z(d, _):
+        def is_far(d):
             source = (z + n_z - d) % n_z
-            far = ((z == 0) & (source == top)) | ((z == top) & (source == 0))
-
-            @pl.when(jnp.logical_not(far & relays))
+            return (((z == 0) & (source == top)) | ((z == top) & (source == 0))) & relays
+
+        def wait_z(d, _):
+            @pl.when(jnp.logical_not(is_far(d)))
             def _():
-                own[k] += received(k, d)
-
-            return 0
-
-        lax.fori_loop(1, n_z, add_z, 0)
-        total = own[k]
+                arrive(k, d)
+
+            return 0
+
+        def add_z(d, total):
+            far = is_far(d)
+            return total + jnp.where(far, 0.0, decoded(k, jnp.where(far, 2, d)))
+
+        lax.fori_loop(1, n_z, wait_z, 0)
+        total = lax.fori_loop(1, n_z, add_z, own[k], unroll=min(n_z - 1, 4))
         high = total.astype(jnp.bfloat16)
         low = (total - high.astype(jnp.float32)).astype(jnp.bfloat16)
         dot = functools.partial(jnp.dot, preferred_element_type=jnp.float32)
@@ -268,15 +276,18 @@
             high = value.astype(jnp.bfloat16)
             rhs[j, :, :LANES] = high
             rhs[j, :, LANES:] = (value - high.astype(jnp.float32)).astype(jnp.bfloat16)
-            return 0
-
-        lax.fori_loop(0, n_row, decode, 0)
+            block = c * n_row + j - r * n_col
+            inside = (block >= 0) & (block < n_col)
+            sums[jnp.where(inside, block, n_col + slots)] = value
+            return 0
+
+        lax.fori_loop(0, n_row, decode, 0, unroll=4)
 
         def products(g, _):
             for u in range(GROUP):
                 s = g * GROUP + u
                 both = jnp.dot(tiles[s], rhs[ids[1, s]], preferred_element_type=jnp.float32)
-                sums[s + 1] = both[:, :LANES] + both[:, LANES:] + sums[prevs[s]]
+                sums[n_col + s] = both[:, :LANES] + both[:, LANES:] + sums[prevs[s]]
             return 0
 
         lax.fori_loop(0, slots // GROUP, products, 0)
@@ -284,17 +295,11 @@
         def hand_over(t, _):
             d = distance(t)
             zz = (z + d) % n_z
-            xs[k, d] = local_block(zz * CORES + other)
+            xs[k, d] = sums[last[zz * CORES + other]]
             core_copy(k, d).start()
             return 0
 
         lax.fori_loop(1, n_z + 1, hand_over, 0)
-
-        def keep(d, _):
-            mine[d] = local_block((z + d) % n_z * CORES + core)
-            return 0
-
-        lax.fori_loop(1, n_z + 1, keep, 0)
 
         @pl.when(k == 0)
         def _():
@@ -308,30 +313,44 @@
         def _():
             project(k - 2)
 
-        def send_z(t, _):
+        def route(t):
             d = distance(t)
             zz = (z + d) % n_z
-            core_copy(k, d).wait_recv()
-            value = mine[d] + xr[k, d]
             from_low = (z == 0) & (zz == top) & relays
             from_high = (z == top) & (zz == 0) & relays
             held = (((z == 1) & (zz == top)) | ((z == top - 1) & (zz == 0))) & relays
-
-            @pl.when(held)
-            def _():
-                xr[k, d] = value
+            slot = jnp.where(from_low, n_z, jnp.where(from_high, n_z + 1, d))
+            target = jnp.where(from_low, 1, jnp.where(from_high, top - 1, zz))
+            return d, zz, slot, target, held
+
+        def wait_core(t, _):
+            core_copy(k, t).wait_recv()
+            return 0
+
+        lax.fori_loop(1, n_z + 1, wait_core, 0)
+
+        def code_z(t, _):
+            d, zz, slot, target, held = route(t)
+            value = sums[last[zz * CORES + core]] + xr[k, d]
+            kept[k, d] = value
+            encode(k, slot, value)
+            return 0
+
+        def send_z(t, _):
+            d, zz, slot, target, held = route(t)
 
             @pl.when(jnp.logical_not(held))
             def _():
-                slot = jnp.where(from_low, n_z, jnp.where(from_high, n_z + 1, d))
-                target = jnp.where(from_low, 1, jnp.where(from_high, top - 1, zz))
-                transmit(k, slot, target, value)
-
-            return 0
-
-        lax.fori_loop(1, n_z, send_z, 0)
-        core_copy(k, n_z).wait_recv()
-        own[k] = mine[n_z] + xr[k, n_z]
+                for copy in z_copies(k, slot, target):
+                    copy.start()
+
+            return 0
+
+        code_z(1, 0)
+        send_z(1, 0)
+        lax.fori_loop(2, n_z, code_z, 0, unroll=min(n_z - 2, 4))
+        lax.fori_loop(2, n_z, send_z, 0)
+        own[k] = sums[last[c]] + xr[k, n_z]
         return 0
 
     row_sums()
@@ -347,7 +366,7 @@
             gscale[j, h * LANES : (h + 1) * LANES, :] = to_columns(gs[j, h : h + 1, :])
         return 0
 
-    lax.fori_loop(0, n_row, spread_scale, 0)
+    lax.fori_loop(0, n_row, spread_scale, 0, unroll=4)
     out_ref[...] = jnp.zeros(out_ref.shape, jnp.float32)
     lax.fori_loop(0, chunks, one_chunk, 0)
 
@@ -435,8 +454,8 @@
                 pltpu.VMEM((n_row, halves, LANES), f32),
                 pltpu.VMEM((n_row, rows, LANES), f32),
                 pltpu.VMEM((n_row, rows, 2 * LANES), bf16),
-                pltpu.VMEM((slots + 1, edge, LANES), f32),
-                pltpu.VMEM((slots + 1, edge, LANES), f32),
+                pltpu.VMEM((n_col + slots + 1, edge, LANES), f32),
+                pltpu.VMEM((n_col + slots + 1, edge, LANES), f32),
                 pltpu.VMEM((chunks, n_z + 1, rows, LANES), f32),
                 pltpu.VMEM((chunks, n_z + 1, rows, LANES), f32),
                 pltpu.VMEM((chunks, n_z + 2, rows, LANES), i16),
@@ -444,7 +463,7 @@
                 pltpu.VMEM((chunks, n_z + 2, rows, LANES), i16),
                 pltpu.VMEM((chunks, n_z + 2, halves, LANES), f32),
                 pltpu.VMEM((chunks, rows, LANES), f32),
-                pltpu.VMEM((n_z + 1, rows, LANES), f32),
+                pltpu.VMEM((chunks, n_z, rows, LANES), f32),
                 pltpu.VMEM((n_col, halves, LANES), f32),
                 pltpu.VMEM((n_col, halves, LANES), f32),
                 pltpu.SMEM((n_col,), jnp.int32),

time: 41.3 us -> 41.8 us (1.012)
  Pallas kernels: 38.6 us -> 39.1 us
    pallas_call x1, Pallas kernels: 38.6 us -> 39.1 us  [shards(): pl.pallas_call(functools.partial(kernel, n_row, n_col, chunks, slots), ou...]
where the time goes in v5:
time: 41.8 us; the launch traced here: 41.6 us
  Pallas kernels  39.1 us (94%)
  local copies, waits for them, and re-layouts  1.87 us (4%)
  between operations  0.66 us (2%)
    pallas_call x1, Pallas kernels, shards(): pl.pallas_call(functools.partial(kernel, n_row, n_col, chunks, slots), ou...  39.1 us
    unnamed x1, local copies, waits for them, and re-layouts  1.87 us

profile of v5, /device:TPU:0, one launch (start us, length us, event | category | flops | bytes accessed | tf_op | source)
XLA Modules:
  0.0 41.6 jit_solution(9803609293615700382)
XLA Ops:
  0.7 39.1 %shard_map.55 = f32[256,512]{1,0:T(8,128)} custom-call(f32[256,512]{1,0:T(8,128)} %feat_hbm.1, f32[512,512]{1,0:T(8,128)} %w_hbm.1, bf16[32,256,256]{2,1,0:T(8,128)(2,1)} %bitcast.4, s32[2,32]{1,0:T(2,128)} %bitcast.5, s32[1,1]{1,0:T(1,128)S(6)} %copy.7.count), custom_call_target="tpu_custom_call" | custom-call | tf_op jit(solution)/shard_map/pallas_call | solution.py:442
  39.8 1.9 %copy.8 = f32[256,512]{1,0:T(8,128)} copy(f32[256,512]{1,0:T(8,128)} %shard_map.55) | data formatting | bytes 1048576

commit v6 on v5

--- a/solution.py
+++ b/solution.py
@@ -10,6 +10,7 @@
 LANES = 128
 CORES = 2
 GROUP = 32
+AHEAD = 2
 QMAX = 32767.0
 MESH = pl.DeviceIdType.MESH
 
@@ -123,7 +124,8 @@
 
         lax.fori_loop(1, n_row, send, 0)
 
-    send_gather(0)
+    for k in range(min(AHEAD, chunks)):
+        send_gather(k)
 
     lax.fori_loop(0, slots, link, 0)
 
@@ -267,9 +269,9 @@
 
         lax.fori_loop(1, n_row, wait_gather, 0)
 
-        @pl.when(k + 1 < chunks)
+        @pl.when(k + AHEAD < chunks)
         def _():
-            send_gather(k + 1)
+            send_gather(k + AHEAD)
 
         def decode(j, _):
             value = gq[j, k].astype(jnp.int32).astype(jnp.float32) * gscale[j]

time: 41.8 us -> 42.1 us (level)
  no operation moved by 1% of the time
where the time goes in v6:
time: 42.1 us; the launch traced here: 41.9 us
  Pallas kernels  39.4 us (94%)
  local copies, waits for them, and re-layouts  1.87 us (4%)
  between operations  0.66 us (2%)
    pallas_call x1, Pallas kernels, shards(): pl.pallas_call(functools.partial(kernel, n_row, n_col, chunks, slots), ou...  39.4 us
    unnamed x1, local copies, waits for them, and re-layouts  1.87 us

profile of v6, /device:TPU:0, one launch (start us, length us, event | category | flops | bytes accessed | tf_op | source)
XLA Modules:
  0.0 41.9 jit_solution(7867245846197966943)
XLA Ops:
  0.7 39.4 %shard_map.55 = f32[256,512]{1,0:T(8,128)} custom-call(f32[256,512]{1,0:T(8,128)} %feat_hbm.1, f32[512,512]{1,0:T(8,128)} %w_hbm.1, bf16[32,256,256]{2,1,0:T(8,128)(2,1)} %bitcast.4, s32[2,32]{1,0:T(2,128)} %bitcast.5, s32[1,1]{1,0:T(1,128)S(6)} %copy.7.count), custom_call_target="tpu_custom_call" | custom-call | tf_op jit(solution)/shard_map/pallas_call | solution.py:444
  40.0 1.9 %copy.8 = f32[256,512]{1,0:T(8,128)} copy(f32[256,512]{1,0:T(8,128)} %shard_map.55) | data formatting | bytes 1048576

commit v7 on v6

--- a/solution.py
+++ b/solution.py
@@ -10,7 +10,7 @@
 LANES = 128
 CORES = 2
 GROUP = 32
-AHEAD = 2
+AHEAD = 1
 QMAX = 32767.0
 MESH = pl.DeviceIdType.MESH
 
@@ -130,6 +130,8 @@
     lax.fori_loop(0, slots, link, 0)
 
     load_t.wait()
+    for i in range(n_col):
+        sums[i] = jnp.zeros(sums.shape[1:], jnp.float32)
 
     def degree_copy(d):
         return pltpu.make_async_remote_copy(
@@ -189,7 +191,7 @@
     def row_sums():
         for i in range(n_col):
             degs[i] = jnp.zeros(degs.shape[1:], jnp.float32)
-            sums[i] = jnp.zeros(sums.shape[1:], jnp.float32)
+
 
         def degree_slot(s, _):
             tile = tiles[s].astype(jnp.float32)
@@ -303,7 +305,7 @@
 
         lax.fori_loop(1, n_z + 1, hand_over, 0)
 
-        @pl.when(k == 0)
+        @pl.when(k == 1)
         def _():
             split_weight()
 
@@ -355,8 +357,6 @@
         own[k] = sums[last[c]] + xr[k, n_z]
         return 0
 
-    row_sums()
-
     def wait_scale(d, _):
         scale_copy(d, (r + n_row - d) % n_row).wait_recv()
         return 0
@@ -372,6 +372,11 @@
     out_ref[...] = jnp.zeros(out_ref.shape, jnp.float32)
     lax.fori_loop(0, chunks, one_chunk, 0)
 
+    row_sums()
+    relay(chunks - 1)
+    for k in range(max(chunks - 2, 0), chunks):
+        project(k)
+
     def add_degree(d, total):
         degree_copy(d).wait_recv()
         return total + dr[d]
@@ -379,9 +384,6 @@
     degree = lax.fori_loop(1, n_col, add_degree, 1.0 + ds[c])
     root = lax.rsqrt(degree)
 
-    relay(chunks - 1)
-    for k in range(max(chunks - 2, 0), chunks):
-        project(k)
     for h in range(halves):
         part = slice(h * LANES, (h + 1) * LANES)
         factor = to_columns(root[h : h + 1, :])

time: 42.1 us -> 42 us (level)
  no operation moved by 1% of the time
where the time goes in v7:
time: 42 us; the launch traced here: 41.8 us
  Pallas kernels  39.3 us (94%)
  local copies, waits for them, and re-layouts  1.87 us (4%)
  between operations  0.66 us (2%)
    pallas_call x1, Pallas kernels, shards(): pl.pallas_call(functools.partial(kernel, n_row, n_col, chunks, slots), ou...  39.3 us
    unnamed x1, local copies, waits for them, and re-layouts  1.87 us

profile of v7, /device:TPU:0, one launch (start us, length us, event | category | flops | bytes accessed | tf_op | source)
XLA Modules:
  0.0 41.8 jit_solution(6884615995878491692)
XLA Ops:
  0.7 39.3 %shard_map.55 = f32[256,512]{1,0:T(8,128)} custom-call(f32[256,512]{1,0:T(8,128)} %feat_hbm.1, f32[512,512]{1,0:T(8,128)} %w_hbm.1, bf16[32,256,256]{2,1,0:T(8,128)(2,1)} %bitcast.4, s32[2,32]{1,0:T(2,128)} %bitcast.5, s32[1,1]{1,0:T(1,128)S(6)} %copy.7.count), custom_call_target="tpu_custom_call" | custom-call | tf_op jit(solution)/shard_map/pallas_call | solution.py:446
  39.9 1.9 %copy.8 = f32[256,512]{1,0:T(8,128)} copy(f32[256,512]{1,0:T(8,128)} %shard_map.55) | data formatting | bytes 1048576

commit v8 on v7

--- a/solution.py
+++ b/solution.py
@@ -39,7 +39,7 @@
 def kernel(
     n_row, n_col, chunks, slots,
     feat_hbm, w_hbm, tiles_hbm, ids, count,
-    out_ref,
+    out_ref, root_ref,
     feat, weight, tiles, w_hi, w_lo,
     gq, gs, gscale, rhs, sums, degs,
     xs, xr, zq, zs, zr, zrs, own, kept, ds, dr,
@@ -327,21 +327,12 @@
             target = jnp.where(from_low, 1, jnp.where(from_high, top - 1, zz))
             return d, zz, slot, target, held
 
-        def wait_core(t, _):
-            core_copy(k, t).wait_recv()
-            return 0
-
-        lax.fori_loop(1, n_z + 1, wait_core, 0)
-
         def code_z(t, _):
             d, zz, slot, target, held = route(t)
+            core_copy(k, d).wait_recv()
             value = sums[last[zz * CORES + core]] + xr[k, d]
             kept[k, d] = value
             encode(k, slot, value)
-            return 0
-
-        def send_z(t, _):
-            d, zz, slot, target, held = route(t)
 
             @pl.when(jnp.logical_not(held))
             def _():
@@ -350,12 +341,12 @@
 
             return 0
 
-        code_z(1, 0)
-        send_z(1, 0)
-        lax.fori_loop(2, n_z, code_z, 0, unroll=min(n_z - 2, 4))
-        lax.fori_loop(2, n_z, send_z, 0)
+        lax.fori_loop(1, n_z, code_z, 0)
+        core_copy(k, n_z).wait_recv()
         own[k] = sums[last[c]] + xr[k, n_z]
         return 0
+
+    row_sums()
 
     def wait_scale(d, _):
         scale_copy(d, (r + n_row - d) % n_row).wait_recv()
@@ -372,7 +363,6 @@
     out_ref[...] = jnp.zeros(out_ref.shape, jnp.float32)
     lax.fori_loop(0, chunks, one_chunk, 0)
 
-    row_sums()
     relay(chunks - 1)
     for k in range(max(chunks - 2, 0), chunks):
         project(k)
@@ -382,14 +372,7 @@
         return total + dr[d]
 
     degree = lax.fori_loop(1, n_col, add_degree, 1.0 + ds[c])
-    root = lax.rsqrt(degree)
-
-    for h in range(halves):
-        part = slice(h * LANES, (h + 1) * LANES)
-        factor = to_columns(root[h : h + 1, :])
-        for k in range(chunks):
-            cols = slice(k * LANES, (k + 1) * LANES)
-            out_ref[part, cols] = jnp.maximum(out_ref[part, cols] * factor, 0.0)
+    root_ref[...] = lax.rsqrt(degree)
 
     def drain_row(d, _):
         scale_copy(d, r).wait_send()
@@ -427,6 +410,15 @@
     lax.fori_loop(1, n_row, drain_row, 0)
     lax.fori_loop(1, n_col, drain_degree, 0)
     lax.fori_loop(0, chunks, drain_core, 0)
+
+
+def finish(sum_ref, root_ref, out_ref):
+    for h in range(out_ref.shape[0] // LANES):
+        part = slice(h * LANES, (h + 1) * LANES)
+        factor = to_columns(root_ref[h : h + 1, :])
+        for k in range(out_ref.shape[1] // LANES):
+            cols = slice(k * LANES, (k + 1) * LANES)
+            out_ref[part, cols] = jnp.maximum(sum_ref[part, cols] * factor, 0.0)
 
 
 def solution(mesh):
@@ -443,11 +435,14 @@
         hbm = pl.BlockSpec(memory_space=pl.ANY)
         smem = pl.BlockSpec(memory_space=pltpu.SMEM)
         vmem = pl.BlockSpec(memory_space=pltpu.VMEM)
-        return pl.pallas_call(
+        summed, root = pl.pallas_call(
             functools.partial(kernel, n_row, n_col, chunks, slots),
-            out_shape=jax.ShapeDtypeStruct((rows, width), f32),
+            out_shape=(
+                jax.ShapeDtypeStruct((rows, width), f32),
+                jax.ShapeDtypeStruct((halves, LANES), f32),
+            ),
             in_specs=[hbm, hbm, hbm, smem, smem],
-            out_specs=vmem,
+            out_specs=(vmem, vmem),
             scratch_shapes=[
                 pltpu.VMEM((rows, width), f32),
                 pltpu.VMEM((width, width), f32),
@@ -496,6 +491,12 @@
             tile_ids.reshape(slots, 2).T,
             tile_counts,
         )
+        return pl.pallas_call(
+            finish,
+            out_shape=jax.ShapeDtypeStruct((rows, width), f32),
+            in_specs=[vmem, vmem],
+            out_specs=vmem,
+        )(summed, root)
 
     in_specs = (
         P(("col", "row"), None),

time: 42 us -> 41.3 us (0.983)
  local copies, waits for them, and re-layouts: 1.87 us -> 0 us
  Pallas kernels: 39.3 us -> 40.5 us
    pallas_call x0 -> x1, Pallas kernels: none -> 1.94 us  [shards(): pl.pallas_call(finish, out_shape=jax.ShapeDtypeStruct((rows, width), f32)...]
    unnamed x1 -> x0, local copies, waits for them, and re-layouts: 1.87 us -> none
    pallas_call x1, Pallas kernels: 39.3 us -> 38.6 us  [shards(): pl.pallas_call(functools.partial(kernel, n_row, n_col, chunks, slots), ou...]
where the time goes in v8:
time: 41.3 us; the launch traced here: 41.2 us
  Pallas kernels  40.5 us (98%)
  between operations  0.66 us (2%)
    pallas_call x1, Pallas kernels, shards(): pl.pallas_call(functools.partial(kernel, n_row, n_col, chunks, slots), ou...  38.6 us
    pallas_call x1, Pallas kernels, shards(): pl.pallas_call(finish, out_shape=jax.ShapeDtypeStruct((rows, width), f32)...  1.94 us

profile of v8, /device:TPU:0, one launch (start us, length us, event | category | flops | bytes accessed | tf_op | source)
XLA Modules:
  0.0 41.2 jit_solution(15468482445987658450)
XLA Ops:
  0.7 38.6 %shard_map.55 = (f32[256,512]{1,0:T(8,128)}, f32[2,128]{1,0:T(2,128)}) custom-call(f32[256,512]{1,0:T(8,128)} %feat_hbm.1, f32[512,512]{1,0:T(8,128)} %w_hbm.1, bf16[32,256,256]{2,1,0:T(8,128)(2,1)} %bitcast.4, s32[2,32]{1,0:T(2,128)} %bitcast.5, s32[1,1]{1,0:T(1,128)S(6)} %copy.6.count), custom_call_target="tpu_custom_call" | custom-call | tf_op jit(solution)/shard_map/pallas_call | solution.py:438
  39.2 1.9 %shard_map.56 = f32[256,512]{1,0:T(8,128)} custom-call(f32[256,512]{1,0:T(8,128)} %get-tuple-element.7.sum_ref, f32[2,128]{1,0:T(2,128)} %get-tuple-element.8.root_ref), custom_call_target="tpu_custom_call" | custom-call | tf_op jit(solution)/shard_map/pallas_call | solution.py:494

commit v9 on v8

--- a/solution.py
+++ b/solution.py
@@ -264,59 +264,7 @@
         dot = functools.partial(jnp.dot, preferred_element_type=jnp.float32)
         out_ref[...] += dot(high, w_hi[k]) + (dot(high, w_lo[k]) + dot(low, w_hi[k]))
 
-    def one_chunk(k, _):
-        def wait_gather(d, _):
-            gather_copy(k, d, (r + n_row - d) % n_row).wait_recv()
-            return 0
-
-        lax.fori_loop(1, n_row, wait_gather, 0)
-
-        @pl.when(k + AHEAD < chunks)
-        def _():
-            send_gather(k + AHEAD)
-
-        def decode(j, _):
-            value = gq[j, k].astype(jnp.int32).astype(jnp.float32) * gscale[j]
-            high = value.astype(jnp.bfloat16)
-            rhs[j, :, :LANES] = high
-            rhs[j, :, LANES:] = (value - high.astype(jnp.float32)).astype(jnp.bfloat16)
-            block = c * n_row + j - r * n_col
-            inside = (block >= 0) & (block < n_col)
-            sums[jnp.where(inside, block, n_col + slots)] = value
-            return 0
-
-        lax.fori_loop(0, n_row, decode, 0, unroll=4)
-
-        def products(g, _):
-            for u in range(GROUP):
-                s = g * GROUP + u
-                both = jnp.dot(tiles[s], rhs[ids[1, s]], preferred_element_type=jnp.float32)
-                sums[n_col + s] = both[:, :LANES] + both[:, LANES:] + sums[prevs[s]]
-            return 0
-
-        lax.fori_loop(0, slots // GROUP, products, 0)
-
-        def hand_over(t, _):
-            d = distance(t)
-            zz = (z + d) % n_z
-            xs[k, d] = sums[last[zz * CORES + other]]
-            core_copy(k, d).start()
-            return 0
-
-        lax.fori_loop(1, n_z + 1, hand_over, 0)
-
-        @pl.when(k == 1)
-        def _():
-            split_weight()
-
-        @pl.when(k >= 1)
-        def _():
-            relay(k - 1)
-
-        @pl.when(k >= 2)
-        def _():
-            project(k - 2)
-
+    def post(k):
         def route(t):
             d = distance(t)
             zz = (z + d) % n_z
@@ -330,7 +278,7 @@
         def code_z(t, _):
             d, zz, slot, target, held = route(t)
             core_copy(k, d).wait_recv()
-            value = sums[last[zz * CORES + core]] + xr[k, d]
+            value = kept[k, d] + xr[k, d]
             kept[k, d] = value
             encode(k, slot, value)
 
@@ -343,7 +291,73 @@
 
         lax.fori_loop(1, n_z, code_z, 0)
         core_copy(k, n_z).wait_recv()
-        own[k] = sums[last[c]] + xr[k, n_z]
+        own[k] = kept[k, n_z] + xr[k, n_z]
+
+    def one_chunk(k, _):
+        def wait_gather(d, _):
+            gather_copy(k, d, (r + n_row - d) % n_row).wait_recv()
+            return 0
+
+        lax.fori_loop(1, n_row, wait_gather, 0)
+
+        @pl.when(k + AHEAD < chunks)
+        def _():
+            send_gather(k + AHEAD)
+
+        def decode(j, _):
+            value = gq[j, k].astype(jnp.int32).astype(jnp.float32) * gscale[j]
+            high = value.astype(jnp.bfloat16)
+            rhs[j, :, :LANES] = high
+            rhs[j, :, LANES:] = (value - high.astype(jnp.float32)).astype(jnp.bfloat16)
+            block = c * n_row + j - r * n_col
+            inside = (block >= 0) & (block < n_col)
+            sums[jnp.where(inside, block, n_col + slots)] = value
+            return 0
+
+        lax.fori_loop(0, n_row, decode, 0, unroll=4)
+
+        def products(g, _):
+            for u in range(GROUP):
+                s = g * GROUP + u
+                both = jnp.dot(tiles[s], rhs[ids[1, s]], preferred_element_type=jnp.float32)
+                sums[n_col + s] = both[:, :LANES] + both[:, LANES:] + sums[prevs[s]]
+            return 0
+
+        lax.fori_loop(0, slots // GROUP, products, 0)
+
+        def hand_over(t, _):
+            d = distance(t)
+            zz = (z + d) % n_z
+            xs[k, d] = sums[last[zz * CORES + other]]
+            core_copy(k, d).start()
+            return 0
+
+        lax.fori_loop(1, n_z + 1, hand_over, 0)
+
+        def keep(t, _):
+            d = distance(t)
+            kept[k, d] = sums[last[(z + d) % n_z * CORES + core]]
+            return 0
+
+        lax.fori_loop(1, n_z + 1, keep, 0)
+
+        @pl.when(k == 0)
+        def _():
+            post(0)
+
+        @pl.when(k == 1)
+        def _():
+            split_weight()
+
+        @pl.when(k >= 2)
+        def _():
+            post(k - 1)
+            relay(k - 2)
+
+        @pl.when(k >= 3)
+        def _():
+            project(k - 3)
+
         return 0
 
     row_sums()
@@ -363,6 +377,13 @@
     out_ref[...] = jnp.zeros(out_ref.shape, jnp.float32)
     lax.fori_loop(0, chunks, one_chunk, 0)
 
+    if chunks == 1:
+        split_weight()
+    else:
+        post(chunks - 1)
+        relay(chunks - 2)
+    if chunks >= 3:
+        project(chunks - 3)
     relay(chunks - 1)
     for k in range(max(chunks - 2, 0), chunks):
         project(k)
@@ -462,7 +483,7 @@
                 pltpu.VMEM((chunks, n_z + 2, rows, LANES), i16),
                 pltpu.VMEM((chunks, n_z + 2, halves, LANES), f32),
                 pltpu.VMEM((chunks, rows, LANES), f32),
-                pltpu.VMEM((chunks, n_z, rows, LANES), f32),
+                pltpu.VMEM((chunks, n_z + 1, rows, LANES), f32),
                 pltpu.VMEM((n_col, halves, LANES), f32),
                 pltpu.VMEM((n_col, halves, LANES), f32),
                 pltpu.SMEM((n_col,), jnp.int32),

time: 41.3 us -> 43.2 us (1.046)
  Pallas kernels: 40.5 us -> 42.4 us
    pallas_call x1, Pallas kernels: 38.6 us -> 40.4 us  [shards(): pl.pallas_call(functools.partial(kernel, n_row, n_col, chunks, slots), ou...]
where the time goes in v9:
time: 43.2 us; the launch traced here: 43 us
  Pallas kernels  42.4 us (98%)
  between operations  0.66 us (2%)
    pallas_call x1, Pallas kernels, shards(): pl.pallas_call(functools.partial(kernel, n_row, n_col, chunks, slots), ou...  40.4 us
    pallas_call x1, Pallas kernels, shards(): pl.pallas_call(finish, out_shape=jax.ShapeDtypeStruct((rows, width), f32)...  1.94 us

profile of v9, /device:TPU:0, one launch (start us, length us, event | category | flops | bytes accessed | tf_op | source)
XLA Modules:
  0.0 43.0 jit_solution(1452962567290181149)
XLA Ops:
  0.7 40.4 %shard_map.55 = (f32[256,512]{1,0:T(8,128)}, f32[2,128]{1,0:T(2,128)}) custom-call(f32[256,512]{1,0:T(8,128)} %feat_hbm.1, f32[512,512]{1,0:T(8,128)} %w_hbm.1, bf16[32,256,256]{2,1,0:T(8,128)(2,1)} %bitcast.4, s32[2,32]{1,0:T(2,128)} %bitcast.5, s32[1,1]{1,0:T(1,128)S(6)} %copy.6.count), custom_call_target="tpu_custom_call" | custom-call | tf_op jit(solution)/shard_map/pallas_call | solution.py:459
  41.1 1.9 %shard_map.56 = f32[256,512]{1,0:T(8,128)} custom-call(f32[256,512]{1,0:T(8,128)} %get-tuple-element.7.sum_ref, f32[2,128]{1,0:T(2,128)} %get-tuple-element.8.root_ref), custom_call_target="tpu_custom_call" | custom-call | tf_op jit(solution)/shard_map/pallas_call | solution.py:515
